TPU v7x, 256 devices: a whole 4x4x8 slice. The times are simulated.
256 devices in a mesh: gx: 16 (over z_lo, x), gy: 4 (over z_hi, core), gz: 4 (over y).
Axes of the slice: x: 4, y: 4, z: 8 (z_hi: 2, z_lo: 4; z = z_hi * 4 + z_lo), core: 2. Of those that a mesh axis runs over, the one named last changes fastest.
Arguments:
- residual: float32 [128, 128, 8192], P('gy', 'gz', 'gx'), may hold values from -11 to 11, as said below
Outputs:
- correction: float32 [128, 128, 8192], P('gy', 'gz', 'gx')
Inputs may be any that keep to these rules, and one draw needn't show every extreme that they name: `residual`: independent from node to node.
All inputs are finite; a program needn't handle non-finite values.
Results may differ from a plain program's by a relative error of at most 0.0001.
Values sent between devices are 32-bit elements; how exact they have to be, the bound alone decides.
A program may use at most 128 MiB of HBM per device.

v0:
```python
import math

import jax
import jax.numpy as jnp
import numpy as np
from jax import lax
from jax.sharding import PartitionSpec as P

ORDER = 7
MID_ORDER = 3
SMOOTH_STEPS = 2
COARSE_STEPS = 4


HIGHEST_PREC = lax.Precision.HIGHEST


def extended_2(block, sides, width, periodic):
    for axis, dim in sides:
        count = lax.axis_size(axis)
        forward = [(i, i + 1) for i in range(count - 1)]
        if periodic:
            forward.append((count - 1, 0))
        backward = [(target, source) for source, target in forward]
        low = lax.ppermute(
            lax.slice_in_dim(block, block.shape[dim] - width, None, axis=dim), axis, forward
        )
        high = lax.ppermute(lax.slice_in_dim(block, 0, width, axis=dim), axis, backward)
        block = jnp.concatenate([low, block, high], axis=dim)
    return block


def legendre_pair(degree, points):
    previous = np.ones(points.shape)
    current = points.copy()
    for level in range(1, degree):
        following = ((2 * level + 1) * points * current - level * previous) / (level + 1)
        previous = current
        current = following
    return (current, previous)


def gll_table(degree):
    points = np.cos(np.pi * np.arange(degree + 1) / degree)
    for sweep in range(100):
        current, previous = legendre_pair(degree, points)
        points = points - (points * current - previous) / ((degree + 1) * current)
    points = points[::-1].copy()
    current, previous = legendre_pair(degree, points)
    weights = 2.0 / (degree * (degree + 1) * current**2)
    return (points, weights)


def lagrange_matrix(targets, points):
    point_count = len(points)
    matrix = np.ones((len(targets), point_count))
    for column in range(point_count):
        for partner in range(point_count):
            if partner != column:
                matrix[:, column] *= (targets - points[partner]) / (
                    points[column] - points[partner]
                )
    return matrix


def line_stiffness(degree):
    points, weights = gll_table(degree)
    point_count = len(points)
    barycentric = np.array(
        [
            1.0
            / np.prod(
                [
                    points[column] - points[partner]
                    for partner in range(point_count)
                    if partner != column
                ]
            )
            for column in range(point_count)
        ]
    )
    derivative = np.zeros((point_count, point_count))
    for target in range(point_count):
        for column in range(point_count):
            if target != column:
                derivative[target, column] = (
                    barycentric[column] / barycentric[target] / (points[target] - points[column])
                )
        derivative[target, target] = -np.sum(derivative[target])
    return (derivative.T @ (weights[:, None] * derivative), weights)


def assembled_patterns(degree):
    stiffness, weights = line_stiffness(degree)
    indices = np.arange(len(weights))
    diag_pat = stiffness[indices, indices].copy()
    weight_pat = weights.copy()
    row_pat = np.abs(stiffness).sum(axis=1)
    for pattern in (diag_pat, weight_pat, row_pat):
        shared = pattern[0] + pattern[-1]
        pattern[0] = shared
        pattern[-1] = shared
    return (diag_pat, weight_pat, row_pat)


def three_terms(special, weight_pat):
    return (
        special[:, None, None] * weight_pat[None, :, None] * weight_pat[None, None, :]
        + weight_pat[:, None, None] * special[None, :, None] * weight_pat[None, None, :]
        + weight_pat[:, None, None] * weight_pat[None, :, None] * special[None, None, :]
    )


def chebyshev_bound(degree):
    diag_pat, weight_pat, row_pat = assembled_patterns(degree)
    return float(np.max(three_terms(row_pat, weight_pat) / three_terms(diag_pat, weight_pat)))


def pattern_vector(pattern, length):
    return jnp.asarray(np.tile(pattern, length // len(pattern)), jnp.float32)


def inverse_diagonal(target_shape, degree):
    diag_pat, weight_pat, row_pat = assembled_patterns(degree)
    diag_a = pattern_vector(diag_pat, target_shape[0])[:, None, None]
    diag_b = pattern_vector(diag_pat, target_shape[1])[None, :, None]
    diag_p = pattern_vector(diag_pat, target_shape[2])[None, None, :]
    weight_a = pattern_vector(weight_pat, target_shape[0])[:, None, None]
    weight_b = pattern_vector(weight_pat, target_shape[1])[None, :, None]
    weight_p = pattern_vector(weight_pat, target_shape[2])[None, None, :]
    total = (
        diag_a * weight_b * weight_p + weight_a * diag_b * weight_p + weight_a * weight_b * diag_p
    )
    return 1.0 / total


def wall_mask(length, position, parts):
    rows = jnp.arange(length)
    start_wall = (rows == 0) & (position == 0)
    end_wall = (rows == length - 1) & (position == parts - 1)
    return jnp.where(start_wall | end_wall, 0.0, 1.0).astype(jnp.float32)


def device_wall(length_a, length_b):
    first_wall = wall_mask(length_a, lax.axis_index("gy"), lax.axis_size("gy"))
    second_wall = wall_mask(length_b, lax.axis_index("gz"), lax.axis_size("gz"))
    return first_wall[:, None, None] * second_wall[None, :, None]


def edge_masks(length, direction, degree):
    position = jnp.arange(length) % (degree + 1)
    target = [1, 1, 1]
    target[direction] = length
    head_mask = (position == 0).astype(jnp.float32).reshape(target)
    tail_mask = (position == degree).astype(jnp.float32).reshape(target)
    return (head_mask, tail_mask)


def block_matrix(matrix_np, elements, smaller):
    group = math.gcd(elements, max(1, 128 // smaller))
    return jnp.asarray(np.kron(np.eye(group), matrix_np), jnp.float32)


def pipe_apply(vector, block):
    size_a, size_b, size_pipe = vector.shape
    in_width = block.shape[1]
    moved = jnp.einsum(
        "abcj,ij->abci",
        vector.reshape(size_a, size_b, size_pipe // in_width, in_width),
        block,
        precision=HIGHEST_PREC,
    )
    return moved.reshape(size_a, size_b, size_pipe // in_width * block.shape[0])


def local_stiffness(vector, degree):
    per_elem = degree + 1
    stiffness_np, weights_np = line_stiffness(degree)
    stiffness = jnp.asarray(stiffness_np, jnp.float32)
    size_a, size_b, size_pipe = vector.shape
    weight_a = pattern_vector(weights_np, size_a)[:, None, None]
    weight_b = pattern_vector(weights_np, size_b)[None, :, None]
    weight_p = pattern_vector(weights_np, size_pipe)[None, None, :]
    along_a = jnp.einsum(
        "ajbc,Jj->aJbc",
        vector.reshape(size_a // per_elem, per_elem, size_b, size_pipe),
        stiffness,
        precision=HIGHEST_PREC,
    ).reshape(vector.shape)
    along_b = jnp.einsum(
        "abjc,Jj->abJc",
        vector.reshape(size_a, size_b // per_elem, per_elem, size_pipe),
        stiffness,
        precision=HIGHEST_PREC,
    ).reshape(vector.shape)
    along_pipe = pipe_apply(vector, block_matrix(stiffness_np, size_pipe // per_elem, per_elem))
    return (
        along_a * weight_b * weight_p
        + along_b * weight_a * weight_p
        + along_pipe * weight_a * weight_b
    )


def transfer(vector, matrix_np):
    matrix = jnp.asarray(matrix_np, jnp.float32)
    out_nodes, in_nodes = matrix_np.shape
    size_a, size_b, size_pipe = vector.shape
    moved = jnp.einsum(
        "ajbc,Jj->aJbc",
        vector.reshape(size_a // in_nodes, in_nodes, size_b, size_pipe),
        matrix,
        precision=HIGHEST_PREC,
    )
    size_a = size_a // in_nodes * out_nodes
    moved = moved.reshape(size_a, size_b, size_pipe)
    moved = jnp.einsum(
        "abjc,Jj->abJc",
        moved.reshape(size_a, size_b // in_nodes, in_nodes, size_pipe),
        matrix,
        precision=HIGHEST_PREC,
    )
    size_b = size_b // in_nodes * out_nodes
    moved = moved.reshape(size_a, size_b, size_pipe)
    return pipe_apply(
        moved, block_matrix(matrix_np, size_pipe // in_nodes, min(in_nodes, out_nodes))
    )


def step_inner(padded, direction, degree):
    length = padded.shape[direction] - 2
    head_mask, tail_mask = edge_masks(length, direction, degree)
    middle = lax.slice_in_dim(padded, 1, length + 1, axis=direction)
    preceding = lax.slice_in_dim(padded, 0, length, axis=direction)
    following = lax.slice_in_dim(padded, 2, length + 2, axis=direction)
    return middle + head_mask * preceding + tail_mask * following


def widen(vector, extended, direction):
    return jnp.concatenate(
        [
            lax.slice_in_dim(extended, 0, 1, axis=direction),
            vector,
            lax.slice_in_dim(extended, 3, 4, axis=direction),
        ],
        axis=direction,
    )


def end_planes(vector, direction):
    length = vector.shape[direction]
    return jnp.concatenate(
        [
            lax.slice_in_dim(vector, 0, 1, axis=direction),
            lax.slice_in_dim(vector, length - 1, length, axis=direction),
        ],
        axis=direction,
    )


def halo_pipe(vector):
    return extended_2(end_planes(vector, 2), (("gx", 2),), 1, True)


def halo_cross_a(vector):
    return extended_2(end_planes(vector, 0), (("gy", 0),), 1, False)


def halo_cross_b(vector):
    return extended_2(end_planes(vector, 1), (("gz", 1),), 1, False)


def assemble_device(vector, degree, wall):
    combined = step_inner(widen(vector, halo_pipe(vector), 2), 2, degree)
    combined = step_inner(widen(combined, halo_cross_a(combined), 0), 0, degree)
    combined = step_inner(widen(combined, halo_cross_b(combined), 1), 1, degree)
    return combined * wall


def chebyshev(local_residual, steps, degree, assemble, inverse_diag):
    upper_bound = chebyshev_bound(degree)
    lower_bound = upper_bound / 10.0
    center = 0.5 * (upper_bound + lower_bound)
    halfwidth = 0.5 * (upper_bound - lower_bound)
    scaled = center / halfwidth
    ratio_now = 1.0 / scaled
    assembled = assemble(local_residual)
    update = inverse_diag * assembled / center
    solution = update
    for iteration in range(1, steps):
        local_residual = local_residual - local_stiffness(update, degree)
        assembled = assemble(local_residual)
        ratio_next = 1.0 / (2.0 * scaled - ratio_now)
        update = ratio_next * ratio_now * update + 2.0 * ratio_next / halfwidth * (
            inverse_diag * assembled
        )
        solution = solution + update
        ratio_now = ratio_next
    return (solution, local_residual, update)


def local(residual):
    fine_points = gll_table(ORDER)[0]
    mid_points = gll_table(MID_ORDER)[0]
    low_points = gll_table(1)[0]
    lift_mid = lagrange_matrix(fine_points, mid_points)
    lift_low = lagrange_matrix(mid_points, low_points)
    fine_wall = device_wall(residual.shape[0], residual.shape[1])
    fine_inverse = inverse_diagonal(residual.shape, ORDER)

    def fine_assemble(vector):
        return assemble_device(vector, ORDER, fine_wall)

    fine_sol, fine_res, fine_last = chebyshev(
        residual, SMOOTH_STEPS, ORDER, fine_assemble, fine_inverse
    )
    fine_res = fine_res - local_stiffness(fine_last, ORDER)
    mid_rhs = transfer(fine_res, lift_mid.T)
    mid_wall = device_wall(mid_rhs.shape[0], mid_rhs.shape[1])
    mid_inverse = inverse_diagonal(mid_rhs.shape, MID_ORDER)

    def mid_assemble(vector):
        return assemble_device(vector, MID_ORDER, mid_wall)

    mid_sol, mid_res, mid_last = chebyshev(
        mid_rhs, SMOOTH_STEPS, MID_ORDER, mid_assemble, mid_inverse
    )
    mid_res = mid_res - local_stiffness(mid_last, MID_ORDER)
    low_rhs = transfer(mid_res, lift_low.T)
    low_a, low_b, low_pipe = low_rhs.shape
    low_wall = device_wall(low_a, low_b)

    def low_assemble(vector):
        return assemble_device(vector, 1, low_wall)

    low_sol = chebyshev(low_rhs, COARSE_STEPS, 1, low_assemble, inverse_diagonal(low_rhs.shape, 1))[
        0
    ]
    mid_lift = transfer(low_sol, lift_low)
    mid_res = mid_res - local_stiffness(mid_lift, MID_ORDER)
    mid_post = chebyshev(mid_res, SMOOTH_STEPS, MID_ORDER, mid_assemble, mid_inverse)[0]
    mid_total = mid_sol + mid_lift + mid_post
    fine_lift = transfer(mid_total, lift_mid)
    fine_res = fine_res - local_stiffness(fine_lift, ORDER)
    fine_post = chebyshev(fine_res, SMOOTH_STEPS, ORDER, fine_assemble, fine_inverse)[0]
    return fine_sol + fine_lift + fine_post


def solution(mesh):
    placed = (P("gy", "gz", "gx"),)
    return jax.shard_map(
        local, mesh=mesh, in_specs=placed, out_specs=P("gy", "gz", "gx"), check_vma=False
    )
```

profile of v0, /device:TPU:1, one launch (start us, length us, event | category | flops | bytes accessed | tf_op | source)
XLA Modules:
  0.0 532.7 jit_solution(11877686929779420316)
XLA Ops:
  9.1 10.5 %collective-permute-done = f32[32,32,1]{2,1,0:T(8,128)S(1)} collective-permute-done((f32[32,32,1]{2,1,0:T(8,128)S(1)}, f32[32,32,1]{2,1,0:T(8,128)S(1)}, u32[]{:S(2)}, u32[]{:S(2)}) %collective-permute-start) | collective-permute-done | bytes 4128 | tf_op jit(solution)/shard_map/ppermute | solution.py:25
  23.8 9.7 %collective-permute-start.2 = (f32[1,32,512]{2,1,0:T(8,128)S(1)}, f32[1,32,512]{2,1,0:T(8,128)S(1)}, u32[]{:S(2)}, u32[]{:S(2)}) collective-permute-start(f32[1,32,512]{2,1,0:T(8,128)S(1)} %get-tuple-element.29), channel_id=1, source_target_pairs={{0,4},{4,8},{8,12},{1,5},{5,9},{9,13},{2,6},{6,10},{10,14},{3,7},{... | collective-permute-start | bytes 196616 | tf_op jit(solution)/shard_map/ppermute | solution.py:25
  35.5 7.5 %collective-permute-done.3 = f32[1,32,512]{2,1,0:T(8,128)S(1)} collective-permute-done((f32[1,32,512]{2,1,0:T(8,128)S(1)}, f32[1,32,512]{2,1,0:T(8,128)S(1)}, u32[]{:S(2)}, u32[]{:S(2)}) %collective-permute-start.3) | collective-permute-done | bytes 65568 | tf_op jit(solution)/shard_map/ppermute | solution.py:28
  69.7 7.3 %collective-permute-done.6 = f32[32,32,1]{2,1,0:T(8,128)S(1)} collective-permute-done((f32[32,32,1]{2,1,0:T(8,128)S(1)}, f32[32,32,1]{2,1,0:T(8,128)S(1)}, u32[]{:S(2)}, u32[]{:S(2)}) %collective-permute-start.6) | collective-permute-done | bytes 4128 | tf_op jit(solution)/shard_map/ppermute | solution.py:25
  83.7 7.5 %collective-permute-done.9 = f32[1,32,512]{2,1,0:T(8,128)S(1)} collective-permute-done((f32[1,32,512]{2,1,0:T(8,128)S(1)}, f32[1,32,512]{2,1,0:T(8,128)S(1)}, u32[]{:S(2)}, u32[]{:S(2)}) %collective-permute-start.9) | collective-permute-done | bytes 65568 | tf_op jit(solution)/shard_map/ppermute | solution.py:28
  120.0 6.1 %collective-permute-start.13 = (f32[16,16,1]{2,1,0:T(8,128)S(1)}, f32[16,16,1]{2,1,0:T(8,128)S(1)}, u32[]{:S(2)}, u32[]{:S(2)}) collective-permute-start(f32[16,16,1]{2,1,0:T(8,128)S(1)} %get-tuple-element.60), channel_id=1, source_target_pairs={{16,0},{32,16},{48,32},{64,48},{80,64},{96,80},{112,96},{128,112},... | collective-permute-start | bytes 3080 | tf_op jit(solution)/shard_map/ppermute | solution.py:28
  134.8 7.0 %collective-permute-done.15 = f32[1,16,256]{2,1,0:T(8,128)S(1)} collective-permute-done((f32[1,16,256]{2,1,0:T(8,128)S(1)}, f32[1,16,256]{2,1,0:T(8,128)S(1)}, u32[]{:S(2)}, u32[]{:S(2)}) %collective-permute-start.15) | collective-permute-done | bytes 16416 | tf_op jit(solution)/shard_map/ppermute | solution.py:28
  156.6 5.8 %collective-permute-start.19 = (f32[16,16,1]{2,1,0:T(8,128)S(1)}, f32[16,16,1]{2,1,0:T(8,128)S(1)}, u32[]{:S(2)}, u32[]{:S(2)}) collective-permute-start(f32[16,16,1]{2,1,0:T(8,128)S(1)} %get-tuple-element.54), channel_id=1, source_target_pairs={{16,0},{32,16},{48,32},{64,48},{80,64},{96,80},{112,96},{128,112},... | collective-permute-start | bytes 3080 | tf_op jit(solution)/shard_map/ppermute | solution.py:28
  171.8 7.0 %collective-permute-done.21 = f32[1,16,256]{2,1,0:T(8,128)S(1)} collective-permute-done((f32[1,16,256]{2,1,0:T(8,128)S(1)}, f32[1,16,256]{2,1,0:T(8,128)S(1)}, u32[]{:S(2)}, u32[]{:S(2)}) %collective-permute-start.21) | collective-permute-done | bytes 16416 | tf_op jit(solution)/shard_map/ppermute | solution.py:28
  207.1 5.8 %collective-permute-start.25 = (f32[8,8,1]{2,1,0:T(8,128)S(1)}, f32[8,8,1]{2,1,0:T(8,128)S(1)}, u32[]{:S(2)}, u32[]{:S(2)}) collective-permute-start(f32[8,8,1]{2,1,0:T(8,128)S(1)} %get-tuple-element.84), channel_id=1, source_target_pairs={{16,0},{32,16},{48,32},{64,48},{80,64},{96,80},{112,96},{128,112},... | collective-permute-start | bytes 776 | tf_op jit(solution)/shard_map/ppermute | solution.py:28
  219.3 6.9 %collective-permute-done.27 = f32[1,8,128]{2,1,0:T(8,128)S(1)} collective-permute-done((f32[1,8,128]{2,1,0:T(8,128)S(1)}, f32[1,8,128]{2,1,0:T(8,128)S(1)}, u32[]{:S(2)}, u32[]{:S(2)}) %collective-permute-start.27) | collective-permute-done | bytes 4128 | tf_op jit(solution)/shard_map/ppermute | solution.py:28
  238.2 5.8 %collective-permute-start.31 = (f32[8,8,1]{2,1,0:T(8,128)S(1)}, f32[8,8,1]{2,1,0:T(8,128)S(1)}, u32[]{:S(2)}, u32[]{:S(2)}) collective-permute-start(f32[8,8,1]{2,1,0:T(8,128)S(1)} %get-tuple-element.78), channel_id=1, source_target_pairs={{16,0},{32,16},{48,32},{64,48},{80,64},{96,80},{112,96},{128,112},... | collective-permute-start | bytes 776 | tf_op jit(solution)/shard_map/ppermute | solution.py:28
  251.5 6.9 %collective-permute-done.33 = f32[1,8,128]{2,1,0:T(8,128)S(1)} collective-permute-done((f32[1,8,128]{2,1,0:T(8,128)S(1)}, f32[1,8,128]{2,1,0:T(8,128)S(1)}, u32[]{:S(2)}, u32[]{:S(2)}) %collective-permute-start.33) | collective-permute-done | bytes 4128 | tf_op jit(solution)/shard_map/ppermute | solution.py:28
  267.7 5.8 %collective-permute-start.37 = (f32[8,8,1]{2,1,0:T(8,128)S(1)}, f32[8,8,1]{2,1,0:T(8,128)S(1)}, u32[]{:S(2)}, u32[]{:S(2)}) collective-permute-start(f32[8,8,1]{2,1,0:T(8,128)S(1)} %get-tuple-element.72), channel_id=1, source_target_pairs={{16,0},{32,16},{48,32},{64,48},{80,64},{96,80},{112,96},{128,112},... | collective-permute-start | bytes 776 | tf_op jit(solution)/shard_map/ppermute | solution.py:28
  281.1 6.9 %collective-permute-done.39 = f32[1,8,128]{2,1,0:T(8,128)S(1)} collective-permute-done((f32[1,8,128]{2,1,0:T(8,128)S(1)}, f32[1,8,128]{2,1,0:T(8,128)S(1)}, u32[]{:S(2)}, u32[]{:S(2)}) %collective-permute-start.39) | collective-permute-done | bytes 4128 | tf_op jit(solution)/shard_map/ppermute | solution.py:28
  310.6 6.9 %collective-permute-done.45 = f32[1,8,128]{2,1,0:T(8,128)S(1)} collective-permute-done((f32[1,8,128]{2,1,0:T(8,128)S(1)}, f32[1,8,128]{2,1,0:T(8,128)S(1)}, u32[]{:S(2)}, u32[]{:S(2)}) %collective-permute-start.45) | collective-permute-done | bytes 4128 | tf_op jit(solution)/shard_map/ppermute | solution.py:28
  354.4 7.0 %collective-permute-done.51 = f32[1,16,256]{2,1,0:T(8,128)S(1)} collective-permute-done((f32[1,16,256]{2,1,0:T(8,128)S(1)}, f32[1,16,256]{2,1,0:T(8,128)S(1)}, u32[]{:S(2)}, u32[]{:S(2)}) %collective-permute-start.51) | collective-permute-done | bytes 16416 | tf_op jit(solution)/shard_map/ppermute | solution.py:28
  379.1 5.9 %collective-permute-start.55 = (f32[16,16,1]{2,1,0:T(8,128)S(1)}, f32[16,16,1]{2,1,0:T(8,128)S(1)}, u32[]{:S(2)}, u32[]{:S(2)}) collective-permute-start(f32[16,16,1]{2,1,0:T(8,128)S(1)} %get-tuple-element.42), channel_id=1, source_target_pairs={{16,0},{32,16},{48,32},{64,48},{80,64},{96,80},{112,96},{128,112},... | collective-permute-start | bytes 3080 | tf_op jit(solution)/shard_map/ppermute | solution.py:28
  394.5 7.0 %collective-permute-done.57 = f32[1,16,256]{2,1,0:T(8,128)S(1)} collective-permute-done((f32[1,16,256]{2,1,0:T(8,128)S(1)}, f32[1,16,256]{2,1,0:T(8,128)S(1)}, u32[]{:S(2)}, u32[]{:S(2)}) %collective-permute-start.57) | collective-permute-done | bytes 16416 | tf_op jit(solution)/shard_map/ppermute | solution.py:28
  451.1 7.9 %collective-permute-done.60 = f32[32,32,1]{2,1,0:T(8,128)S(1)} collective-permute-done((f32[32,32,1]{2,1,0:T(8,128)S(1)}, f32[32,32,1]{2,1,0:T(8,128)S(1)}, u32[]{:S(2)}, u32[]{:S(2)}) %collective-permute-start.60) | collective-permute-done | bytes 4128 | tf_op jit(solution)/shard_map/ppermute | solution.py:25
  465.2 7.6 %collective-permute-done.63 = f32[1,32,512]{2,1,0:T(8,128)S(1)} collective-permute-done((f32[1,32,512]{2,1,0:T(8,128)S(1)}, f32[1,32,512]{2,1,0:T(8,128)S(1)}, u32[]{:S(2)}, u32[]{:S(2)}) %collective-permute-start.63) | collective-permute-done | bytes 65568 | tf_op jit(solution)/shard_map/ppermute | solution.py:28
  492.1 6.1 %collective-permute-start.67 = (f32[32,32,1]{2,1,0:T(8,128)S(1)}, f32[32,32,1]{2,1,0:T(8,128)S(1)}, u32[]{:S(2)}, u32[]{:S(2)}) collective-permute-start(f32[32,32,1]{2,1,0:T(8,128)S(1)} %get-tuple-element.14), channel_id=1, source_target_pairs={{16,0},{32,16},{48,32},{64,48},{80,64},{96,80},{112,96},{128,112},... | collective-permute-start | bytes 12296 | tf_op jit(solution)/shard_map/ppermute | solution.py:28
  498.2 7.2 %collective-permute-done.66 = f32[32,32,1]{2,1,0:T(8,128)S(1)} collective-permute-done((f32[32,32,1]{2,1,0:T(8,128)S(1)}, f32[32,32,1]{2,1,0:T(8,128)S(1)}, u32[]{:S(2)}, u32[]{:S(2)}) %collective-permute-start.66) | collective-permute-done | bytes 4128 | tf_op jit(solution)/shard_map/ppermute | solution.py:25
  512.1 7.6 %collective-permute-done.69 = f32[1,32,512]{2,1,0:T(8,128)S(1)} collective-permute-done((f32[1,32,512]{2,1,0:T(8,128)S(1)}, f32[1,32,512]{2,1,0:T(8,128)S(1)}, u32[]{:S(2)}, u32[]{:S(2)}) %collective-permute-start.69) | collective-permute-done | bytes 65568 | tf_op jit(solution)/shard_map/ppermute | solution.py:28
  (481 shorter events, 360.4 us)
Async XLA Ops:
  1.4 18.2 %collective-permute-start = (f32[32,32,1]{2,1,0:T(8,128)S(1)}, f32[32,32,1]{2,1,0:T(8,128)S(1)}, u32[]{:S(2)}, u32[]{:S(2)}) collective-permute-start(f32[32,32,1]{2,1,0:T(8,128)S(1)} %get-tuple-element.31), channel_id=1, source_target_pairs={{0,16},{16,32},{32,48},{48,64},{64,80},{80,96},{96,112},{112,128},... | collective-permute-start | bytes 12296 | tf_op jit(solution)/shard_map/ppermute | solution.py:25
  3.6 16.0 %collective-permute-start.1 = (f32[32,32,1]{2,1,0:T(8,128)S(1)}, f32[32,32,1]{2,1,0:T(8,128)S(1)}, u32[]{:S(2)}, u32[]{:S(2)}) collective-permute-start(f32[32,32,1]{2,1,0:T(8,128)S(1)} %get-tuple-element.32), channel_id=1, source_target_pairs={{16,0},{32,16},{48,32},{64,48},{80,64},{96,80},{112,96},{128,112},... | collective-permute-start | bytes 12296 | tf_op jit(solution)/shard_map/ppermute | solution.py:28
  23.8 11.6 %collective-permute-start.2 = (f32[1,32,512]{2,1,0:T(8,128)S(1)}, f32[1,32,512]{2,1,0:T(8,128)S(1)}, u32[]{:S(2)}, u32[]{:S(2)}) collective-permute-start(f32[1,32,512]{2,1,0:T(8,128)S(1)} %get-tuple-element.29), channel_id=1, source_target_pairs={{0,4},{4,8},{8,12},{1,5},{5,9},{9,13},{2,6},{6,10},{10,14},{3,7},{... | collective-permute-start | bytes 196616 | tf_op jit(solution)/shard_map/ppermute | solution.py:25
  33.5 9.5 %collective-permute-start.3 = (f32[1,32,512]{2,1,0:T(8,128)S(1)}, f32[1,32,512]{2,1,0:T(8,128)S(1)}, u32[]{:S(2)}, u32[]{:S(2)}) collective-permute-start(f32[1,32,512]{2,1,0:T(8,128)S(1)} %get-tuple-element.30), channel_id=1, source_target_pairs={{4,0},{8,4},{12,8},{5,1},{9,5},{13,9},{6,2},{10,6},{14,10},{7,3},{... | collective-permute-start | bytes 196616 | tf_op jit(solution)/shard_map/ppermute | solution.py:28
  63.8 13.2 %collective-permute-start.6 = (f32[32,32,1]{2,1,0:T(8,128)S(1)}, f32[32,32,1]{2,1,0:T(8,128)S(1)}, u32[]{:S(2)}, u32[]{:S(2)}) collective-permute-start(f32[32,32,1]{2,1,0:T(8,128)S(1)} %get-tuple-element.25), channel_id=1, source_target_pairs={{0,16},{16,32},{32,48},{48,64},{64,80},{80,96},{96,112},{112,128},... | collective-permute-start | bytes 12296 | tf_op jit(solution)/shard_map/ppermute | solution.py:25
  64.0 13.3 %collective-permute-start.7 = (f32[32,32,1]{2,1,0:T(8,128)S(1)}, f32[32,32,1]{2,1,0:T(8,128)S(1)}, u32[]{:S(2)}, u32[]{:S(2)}) collective-permute-start(f32[32,32,1]{2,1,0:T(8,128)S(1)} %get-tuple-element.26), channel_id=1, source_target_pairs={{16,0},{32,16},{48,32},{64,48},{80,64},{96,80},{112,96},{128,112},... | collective-permute-start | bytes 12296 | tf_op jit(solution)/shard_map/ppermute | solution.py:28
  81.6 9.5 %collective-permute-start.9 = (f32[1,32,512]{2,1,0:T(8,128)S(1)}, f32[1,32,512]{2,1,0:T(8,128)S(1)}, u32[]{:S(2)}, u32[]{:S(2)}) collective-permute-start(f32[1,32,512]{2,1,0:T(8,128)S(1)} %get-tuple-element.24), channel_id=1, source_target_pairs={{4,0},{8,4},{12,8},{5,1},{9,5},{13,9},{6,2},{10,6},{14,10},{7,3},{... | collective-permute-start | bytes 196616 | tf_op jit(solution)/shard_map/ppermute | solution.py:28
  119.9 8.5 %collective-permute-start.12 = (f32[16,16,1]{2,1,0:T(8,128)S(1)}, f32[16,16,1]{2,1,0:T(8,128)S(1)}, u32[]{:S(2)}, u32[]{:S(2)}) collective-permute-start(f32[16,16,1]{2,1,0:T(8,128)S(1)} %get-tuple-element.59), channel_id=1, source_target_pairs={{0,16},{16,32},{32,48},{48,64},{64,80},{80,96},{96,112},{112,128},... | collective-permute-start | bytes 3080 | tf_op jit(solution)/shard_map/ppermute | solution.py:25
  120.0 8.4 %collective-permute-start.13 = (f32[16,16,1]{2,1,0:T(8,128)S(1)}, f32[16,16,1]{2,1,0:T(8,128)S(1)}, u32[]{:S(2)}, u32[]{:S(2)}) collective-permute-start(f32[16,16,1]{2,1,0:T(8,128)S(1)} %get-tuple-element.60), channel_id=1, source_target_pairs={{16,0},{32,16},{48,32},{64,48},{80,64},{96,80},{112,96},{128,112},... | collective-permute-start | bytes 3080 | tf_op jit(solution)/shard_map/ppermute | solution.py:28
  132.8 9.0 %collective-permute-start.15 = (f32[1,16,256]{2,1,0:T(8,128)S(1)}, f32[1,16,256]{2,1,0:T(8,128)S(1)}, u32[]{:S(2)}, u32[]{:S(2)}) collective-permute-start(f32[1,16,256]{2,1,0:T(8,128)S(1)} %get-tuple-element.58), channel_id=1, source_target_pairs={{4,0},{8,4},{12,8},{5,1},{9,5},{13,9},{6,2},{10,6},{14,10},{7,3},{... | collective-permute-start | bytes 49160 | tf_op jit(solution)/shard_map/ppermute | solution.py:28
  169.9 9.0 %collective-permute-start.21 = (f32[1,16,256]{2,1,0:T(8,128)S(1)}, f32[1,16,256]{2,1,0:T(8,128)S(1)}, u32[]{:S(2)}, u32[]{:S(2)}) collective-permute-start(f32[1,16,256]{2,1,0:T(8,128)S(1)} %get-tuple-element.52), channel_id=1, source_target_pairs={{4,0},{8,4},{12,8},{5,1},{9,5},{13,9},{6,2},{10,6},{14,10},{7,3},{... | collective-permute-start | bytes 49160 | tf_op jit(solution)/shard_map/ppermute | solution.py:28
  180.9 8.8 %collective-permute-start.22 = (f32[16,1,256]{2,1,0:T(1,128)}, f32[16,1,256]{2,1,0:T(1,128)}, u32[]{:S(2)}, u32[]{:S(2)}) collective-permute-start(f32[16,1,256]{2,1,0:T(1,128)} %get-tuple-element.49), channel_id=1, source_target_pairs={{0,1},{1,2},{2,3},{4,5},{5,6},{6,7},{8,9},{9,10},{10,11},{12,13},{... | collective-permute-start | bytes 49160 | tf_op jit(solution)/shard_map/ppermute | solution.py:25
  217.4 8.8 %collective-permute-start.27 = (f32[1,8,128]{2,1,0:T(8,128)S(1)}, f32[1,8,128]{2,1,0:T(8,128)S(1)}, u32[]{:S(2)}, u32[]{:S(2)}) collective-permute-start(f32[1,8,128]{2,1,0:T(8,128)S(1)} %get-tuple-element.82), channel_id=1, source_target_pairs={{4,0},{8,4},{12,8},{5,1},{9,5},{13,9},{6,2},{10,6},{14,10},{7,3},{... | collective-permute-start | bytes 12296 | tf_op jit(solution)/shard_map/ppermute | solution.py:28
  249.6 8.8 %collective-permute-start.33 = (f32[1,8,128]{2,1,0:T(8,128)S(1)}, f32[1,8,128]{2,1,0:T(8,128)S(1)}, u32[]{:S(2)}, u32[]{:S(2)}) collective-permute-start(f32[1,8,128]{2,1,0:T(8,128)S(1)} %get-tuple-element.76), channel_id=1, source_target_pairs={{4,0},{8,4},{12,8},{5,1},{9,5},{13,9},{6,2},{10,6},{14,10},{7,3},{... | collective-permute-start | bytes 12296 | tf_op jit(solution)/shard_map/ppermute | solution.py:28
  279.1 8.8 %collective-permute-start.39 = (f32[1,8,128]{2,1,0:T(8,128)S(1)}, f32[1,8,128]{2,1,0:T(8,128)S(1)}, u32[]{:S(2)}, u32[]{:S(2)}) collective-permute-start(f32[1,8,128]{2,1,0:T(8,128)S(1)} %get-tuple-element.70), channel_id=1, source_target_pairs={{4,0},{8,4},{12,8},{5,1},{9,5},{13,9},{6,2},{10,6},{14,10},{7,3},{... | collective-permute-start | bytes 12296 | tf_op jit(solution)/shard_map/ppermute | solution.py:28
  308.7 8.8 %collective-permute-start.45 = (f32[1,8,128]{2,1,0:T(8,128)S(1)}, f32[1,8,128]{2,1,0:T(8,128)S(1)}, u32[]{:S(2)}, u32[]{:S(2)}) collective-permute-start(f32[1,8,128]{2,1,0:T(8,128)S(1)} %get-tuple-element.64), channel_id=1, source_target_pairs={{4,0},{8,4},{12,8},{5,1},{9,5},{13,9},{6,2},{10,6},{14,10},{7,3},{... | collective-permute-start | bytes 12296 | tf_op jit(solution)/shard_map/ppermute | solution.py:28
  352.5 9.0 %collective-permute-start.51 = (f32[1,16,256]{2,1,0:T(8,128)S(1)}, f32[1,16,256]{2,1,0:T(8,128)S(1)}, u32[]{:S(2)}, u32[]{:S(2)}) collective-permute-start(f32[1,16,256]{2,1,0:T(8,128)S(1)} %get-tuple-element.46), channel_id=1, source_target_pairs={{4,0},{8,4},{12,8},{5,1},{9,5},{13,9},{6,2},{10,6},{14,10},{7,3},{... | collective-permute-start | bytes 49160 | tf_op jit(solution)/shard_map/ppermute | solution.py:28
  392.4 9.1 %collective-permute-start.57 = (f32[1,16,256]{2,1,0:T(8,128)S(1)}, f32[1,16,256]{2,1,0:T(8,128)S(1)}, u32[]{:S(2)}, u32[]{:S(2)}) collective-permute-start(f32[1,16,256]{2,1,0:T(8,128)S(1)} %get-tuple-element.40), channel_id=1, source_target_pairs={{4,0},{8,4},{12,8},{5,1},{9,5},{13,9},{6,2},{10,6},{14,10},{7,3},{... | collective-permute-start | bytes 49160 | tf_op jit(solution)/shard_map/ppermute | solution.py:28
  445.2 13.8 %collective-permute-start.60 = (f32[32,32,1]{2,1,0:T(8,128)S(1)}, f32[32,32,1]{2,1,0:T(8,128)S(1)}, u32[]{:S(2)}, u32[]{:S(2)}) collective-permute-start(f32[32,32,1]{2,1,0:T(8,128)S(1)} %get-tuple-element.19), channel_id=1, source_target_pairs={{0,16},{16,32},{32,48},{48,64},{64,80},{80,96},{96,112},{112,128},... | collective-permute-start | bytes 12296 | tf_op jit(solution)/shard_map/ppermute | solution.py:25
  445.3 13.7 %collective-permute-start.61 = (f32[32,32,1]{2,1,0:T(8,128)S(1)}, f32[32,32,1]{2,1,0:T(8,128)S(1)}, u32[]{:S(2)}, u32[]{:S(2)}) collective-permute-start(f32[32,32,1]{2,1,0:T(8,128)S(1)} %get-tuple-element.20), channel_id=1, source_target_pairs={{16,0},{32,16},{48,32},{64,48},{80,64},{96,80},{112,96},{128,112},... | collective-permute-start | bytes 12296 | tf_op jit(solution)/shard_map/ppermute | solution.py:28
  463.2 9.6 %collective-permute-start.63 = (f32[1,32,512]{2,1,0:T(8,128)S(1)}, f32[1,32,512]{2,1,0:T(8,128)S(1)}, u32[]{:S(2)}, u32[]{:S(2)}) collective-permute-start(f32[1,32,512]{2,1,0:T(8,128)S(1)} %get-tuple-element.18), channel_id=1, source_target_pairs={{4,0},{8,4},{12,8},{5,1},{9,5},{13,9},{6,2},{10,6},{14,10},{7,3},{... | collective-permute-start | bytes 196616 | tf_op jit(solution)/shard_map/ppermute | solution.py:28
  492.0 13.4 %collective-permute-start.66 = (f32[32,32,1]{2,1,0:T(8,128)S(1)}, f32[32,32,1]{2,1,0:T(8,128)S(1)}, u32[]{:S(2)}, u32[]{:S(2)}) collective-permute-start(f32[32,32,1]{2,1,0:T(8,128)S(1)} %get-tuple-element.13), channel_id=1, source_target_pairs={{0,16},{16,32},{32,48},{48,64},{64,80},{80,96},{96,112},{112,128},... | collective-permute-start | bytes 12296 | tf_op jit(solution)/shard_map/ppermute | solution.py:25
  492.1 13.4 %collective-permute-start.67 = (f32[32,32,1]{2,1,0:T(8,128)S(1)}, f32[32,32,1]{2,1,0:T(8,128)S(1)}, u32[]{:S(2)}, u32[]{:S(2)}) collective-permute-start(f32[32,32,1]{2,1,0:T(8,128)S(1)} %get-tuple-element.14), channel_id=1, source_target_pairs={{16,0},{32,16},{48,32},{64,48},{80,64},{96,80},{112,96},{128,112},... | collective-permute-start | bytes 12296 | tf_op jit(solution)/shard_map/ppermute | solution.py:28
  510.0 9.6 %collective-permute-start.69 = (f32[1,32,512]{2,1,0:T(8,128)S(1)}, f32[1,32,512]{2,1,0:T(8,128)S(1)}, u32[]{:S(2)}, u32[]{:S(2)}) collective-permute-start(f32[1,32,512]{2,1,0:T(8,128)S(1)} %get-tuple-element.12), channel_id=1, source_target_pairs={{4,0},{8,4},{12,8},{5,1},{9,5},{13,9},{6,2},{10,6},{14,10},{7,3},{... | collective-permute-start | bytes 196616 | tf_op jit(solution)/shard_map/ppermute | solution.py:28
  (139 other events, 2765.9 us)
where the time goes:
time: 539 us; the launch traced here: 533 us
  starting transfers between devices  192 us (36%)
  waiting for transfers between devices  166 us (31%)
  matrix products  78.1 us (14%)
  local copies, waits for them, and re-layouts  54.8 us (10%)
  other arithmetic  39.3 us (7%)
    ppermute x36, waiting for transfers between devices, extended_2(): lax.ppermute(lax.slice_in_dim(block, 0, width, axis=dim), axis, backward)  119 us
    ppermute x36, starting transfers between devices, extended_2(): lax.ppermute(lax.slice_in_dim(block, 0, width, axis=dim), axis, backward)  110 us
    ppermute x36, starting transfers between devices, extended_2(): lax.ppermute(lax.slice_in_dim(block, block.shape[dim] - width, None, axis...  81.8 us
    ppermute x36, waiting for transfers between devices, extended_2(): lax.ppermute(lax.slice_in_dim(block, block.shape[dim] - width, None, axis...  46.9 us
    dot_general x15, matrix products, pipe_apply(): jnp.einsum('abcj,ij->abci', vector.reshape(size_a, size_b, size_pipe // i...  23 us
    dot_general x11, matrix products, local_stiffness(): jnp.einsum('abjc,Jj->abJc', vector.reshape(size_a, size_b // per_elem, pe...  22.7 us
    dot_general x11, matrix products, local_stiffness(): jnp.einsum('ajbc,Jj->aJbc', vector.reshape(size_a // per_elem, per_elem,...  20.5 us
    add x24, other arithmetic, step_inner(): return middle + head_mask * preceding + tail_mask * following  14.5 us
  transfers between devices with their start and end apart: 72, of which 37 were waited for; matrix products, arithmetic and copies ran while one was open for 1% of the time, Pallas kernels for 0%

commit v1 on v0

v1 whole, which is shorter than its diff:
```python
import itertools

import jax
import jax.numpy as jnp
import numpy as np
from jax import lax
from jax.experimental import pallas as pl
from jax.experimental.pallas import tpu as pltpu
from jax.sharding import PartitionSpec as P

ORDER = 7
MID_ORDER = 3
COARSE_STEPS = 4


def legendre_pair(degree, points):
    previous = np.ones(points.shape)
    current = points.copy()
    for level in range(1, degree):
        following = ((2 * level + 1) * points * current - level * previous) / (level + 1)
        previous = current
        current = following
    return (current, previous)


def gll_table(degree):
    points = np.cos(np.pi * np.arange(degree + 1) / degree)
    for sweep in range(100):
        current, previous = legendre_pair(degree, points)
        points = points - (points * current - previous) / ((degree + 1) * current)
    points = points[::-1].copy()
    current, previous = legendre_pair(degree, points)
    weights = 2.0 / (degree * (degree + 1) * current**2)
    return (points, weights)


def lagrange_matrix(targets, points):
    point_count = len(points)
    matrix = np.ones((len(targets), point_count))
    for column in range(point_count):
        for partner in range(point_count):
            if partner != column:
                matrix[:, column] *= (targets - points[partner]) / (
                    points[column] - points[partner]
                )
    return matrix


def line_stiffness(degree):
    points, weights = gll_table(degree)
    point_count = len(points)
    barycentric = np.array(
        [
            1.0
            / np.prod(
                [
                    points[column] - points[partner]
                    for partner in range(point_count)
                    if partner != column
                ]
            )
            for column in range(point_count)
        ]
    )
    derivative = np.zeros((point_count, point_count))
    for target in range(point_count):
        for column in range(point_count):
            if target != column:
                derivative[target, column] = (
                    barycentric[column] / barycentric[target] / (points[target] - points[column])
                )
        derivative[target, target] = -np.sum(derivative[target])
    return (derivative.T @ (weights[:, None] * derivative), weights)


def assembled_patterns(degree):
    stiffness, weights = line_stiffness(degree)
    indices = np.arange(len(weights))
    diag_pat = stiffness[indices, indices].copy()
    weight_pat = weights.copy()
    row_pat = np.abs(stiffness).sum(axis=1)
    for pattern in (diag_pat, weight_pat, row_pat):
        shared = pattern[0] + pattern[-1]
        pattern[0] = shared
        pattern[-1] = shared
    return (diag_pat, weight_pat, row_pat)


def three_terms(special, weight_pat):
    return (
        special[:, None, None] * weight_pat[None, :, None] * weight_pat[None, None, :]
        + weight_pat[:, None, None] * special[None, :, None] * weight_pat[None, None, :]
        + weight_pat[:, None, None] * weight_pat[None, :, None] * special[None, None, :]
    )


def chebyshev_bound(degree):
    diag_pat, weight_pat, row_pat = assembled_patterns(degree)
    return float(np.max(three_terms(row_pat, weight_pat) / three_terms(diag_pat, weight_pat)))


class Level:
    def __init__(self, q):
        stiffness, weights = line_stiffness(q)
        diag_pat, weight_pat, row_pat = assembled_patterns(q)
        self.q = self.n = q
        self.half = half = (q + 1) // 2
        self.mass = weight_pat
        self.gain = gain = stiffness / weight_pat[:, None]
        self.even = 0.5 * (gain[:half, :half] + gain[:half, ::-1][:, :half])
        self.odd = 0.5 * (gain[:half, :half] - gain[:half, ::-1][:, :half])
        self.alpha = diag_pat / weight_pat
        upper = chebyshev_bound(q)
        lower = upper / 10.0
        self.center = 0.5 * (upper + lower)
        self.halfwidth = 0.5 * (upper - lower)

    def inverse(self, a, b, c):
        return 1.0 / (self.alpha[a] + self.alpha[b] + self.alpha[c])

    def factors(self, steps):
        scaled = self.center / self.halfwidth
        ratio = 1.0 / scaled
        found = []
        for step in range(1, steps):
            following = 1.0 / (2.0 * scaled - ratio)
            found.append((following * ratio, 2.0 * following / self.halfwidth))
            ratio = following
        return found


FINE, MID, LOW = Level(ORDER), Level(MID_ORDER), Level(1)
ALL_DIMS = "abc"
SUBSETS = ("a", "b", "c", "ab", "ac", "bc", "abc")
TAB = 33
BLOCKS = [o for o in itertools.product((-1, 0, 1), repeat=3) if any(o)]


def table():
    rows = []
    for a in range(7):
        inverse = [FINE.inverse(a, b, c) for b in range(4) for c in range(4)]
        scale = [
            1.0 / (FINE.mass[a] * FINE.mass[b] * FINE.mass[c]) for b in range(4) for c in range(4)
        ]
        rows += inverse + scale + [FINE.gain[a, 7]]
    return np.asarray(rows, np.float32)


def combo(b, c):
    return min(b, 7 - b) * 4 + min(c, 7 - c)


def node(dim, m, i, k):
    return {"a": (m, i, k), "b": (i, m, k), "c": (i, k, m)}[dim]


def face_vregs(n, dim):
    return 1 if dim == "c" else n * -(-n // 4)


def plan():
    slots, size, count = {}, 0, 0

    def add(key, length):
        nonlocal size, count
        slots[key] = (size, length, count)
        size += length
        count += 1

    for name, n in (
        ("f1", 7), ("f2", 7), ("f3", 7), ("f4", 7),
        ("m1", 3), ("m2", 3), ("m4", 3),
    ):
        for dim in ALL_DIMS:
            for way in (1, -1):
                add((name, dim, way), face_vregs(n, dim))
    for name, n, way in (("S7", 7, 1), ("S3", 3, 1), ("S1", 1, 1), ("C3", 3, -1), ("C7", 7, -1)):
        for dims in SUBSETS:
            add((name, dims, way), face_vregs(n, dims) if len(dims) == 1 else n ** (3 - len(dims)))
    for offset in BLOCKS:
        add(offset, 1)
    return slots, -(-size // 8) * 8, count


SLOTS, BUF_VREGS, MESSAGES = plan()


def total(terms):
    out = None
    for term in terms:
        if term is not None:
            out = term if out is None else out + term
    return out


def mix(coefs, values):
    return total(
        None if abs(coef) < 1e-13 else float(coef) * value for coef, value in zip(coefs, values)
    )


def kernel(sizes, tab, x, out, tr, u, rho, d, xs, w1, w2, ha, pk, sbuf, rbuf, ssem, rsem):
    nx, ny, nz = sizes
    gx, gy, gz = lax.axis_index("gx"), lax.axis_index("gy"), lax.axis_index("gz")
    rows = lax.broadcasted_iota(jnp.int32, (8, 128), 0)
    lanes = lax.broadcasted_iota(jnp.int32, (8, 128), 1)
    odd_row, odd_lane = rows % 2 == 1, lanes % 2 == 1
    first = {"a": rows < 2, "b": (rows % 2 == 0) & (lanes % 2 == 0), "c": lanes < 2}
    last = {"a": rows >= 6, "b": odd_row & odd_lane, "c": lanes >= 126}
    wall_a = jnp.where(first["a"] & (gy == 0), 0.0, 1.0).astype(jnp.float32)
    wall_b = jnp.where(first["b"] & (gz == 0), 0.0, 1.0).astype(jnp.float32)

    def spin(v, row, lane):
        if row % 8:
            v = pltpu.roll(v, row % 8, 0)
        if lane % 128:
            v = pltpu.roll(v, lane % 128, 1)
        return v

    def up(dim, v):
        if dim == "a":
            return jnp.where(rows >= 2, spin(v, 2, 0), 0.0)
        if dim == "b":
            w = jnp.where(odd_lane, jnp.where(odd_row, spin(v, 1, 0), 0.0), v)
            return jnp.where(odd_lane, spin(w, 0, 1), spin(w, 0, -1))
        t = jnp.where(lanes < 8, spin(v, 0, 10), spin(v, 0, 8))
        return jnp.where(lanes < 2, 0.0, t)

    def down(dim, v):
        if dim == "a":
            return jnp.where(rows < 6, spin(v, -2, 0), 0.0)
        if dim == "b":
            w = jnp.where(odd_lane, v, jnp.where(odd_row, 0.0, spin(v, -1, 0)))
            return jnp.where(odd_lane, spin(w, 0, 1), spin(w, 0, -1))
        t = jnp.where(lanes >= 120, spin(v, 0, -10), spin(v, 0, -8))
        return jnp.where(lanes >= 126, 0.0, t)

    def pack(dim, way, vs):
        acc = None
        for j, v in enumerate(vs):
            if dim == "a":
                v, mask = spin(v, 2 * j + (2 if way > 0 else 0), 0), rows // 2 == j
            elif dim == "b":
                js, jl = j % 2, j // 2
                back = 1 if way > 0 else 0
                v, mask = spin(v, js - back, jl - back), (rows % 2 == js) & (lanes % 2 == jl)
            else:
                v, mask = spin(v, 0, 2 * j + (2 if way > 0 else 0)), lanes // 2 == j
            acc = v if acc is None else jnp.where(mask, v, acc)
        return acc

    def unpack(dim, way, w, j):
        if dim == "a":
            w = spin(w, -2 * j if way > 0 else 6 - 2 * j, 0)
        elif dim == "b":
            js, jl = j % 2, j // 2
            w = spin(w, -js, -jl) if way > 0 else spin(w, 1 - js, 1 - jl)
        else:
            w = spin(w, 0, -2 * j if way > 0 else 126 - 2 * j)
        return jnp.where((first if way > 0 else last)[dim], w, 0.0)

    def move(dims, way, v):
        row = (2 if "a" in dims else 0) - (1 if "b" in dims else 0)
        lane = (2 if "c" in dims else 0) - (1 if "b" in dims else 0)
        mask = None
        for dim in dims:
            part = (first if way > 0 else last)[dim]
            mask = part if mask is None else mask & part
        return jnp.where(mask, spin(v, way * row, way * lane), 0.0)

    def guarded(key, way, run):
        name, dims, _ = key
        if name in ("f1", "f2", "f3", "f4", "S7", "C7") and "a" in dims:
            pl.when(gy < ny - 1 if way > 0 else gy > 0)(run)
        else:
            run()

    def device_at(da, db, dc):
        return {
            "gx": lax.rem(gx + dc + nx, nx) if dc else gx,
            "gy": lax.rem(gy + da + ny, ny) if da else gy,
            "gz": lax.rem(gz + db + nz, nz) if db else gz,
        }

    def remote(src, dst, index, device):
        return pltpu.make_async_remote_copy(
            src_ref=src,
            dst_ref=dst,
            send_sem=ssem.at[index],
            recv_sem=rsem.at[index],
            device_id=device,
            device_id_type=pl.DeviceIdType.MESH,
        )

    def copy_of(key):
        name, dims, way = key
        offset, length, index = SLOTS[key]
        part = pl.ds(offset * 8, length * 8)
        device = device_at(*(way if dim in dims else 0 for dim in ALL_DIMS))
        return remote(sbuf.at[part], rbuf.at[part], index, device)

    pending = []

    def send(key):
        guarded(key, key[2], lambda: copy_of(key).start())
        pending.append(key)

    def receive(key):
        guarded(key, -key[2], lambda: copy_of(key).wait_recv())

    def drain(keep=None):
        for key in list(pending):
            if key[0] != keep:
                guarded(key, key[2], lambda: copy_of(key).wait_send())
                pending.remove(key)

    def tile(ref, index):
        start = index * 8
        if not isinstance(index, int):
            start = pl.multiple_of(start, 8)
        return ref[pl.ds(start, 8), :]

    def put(ref, index, value):
        start = index * 8
        if not isinstance(index, int):
            start = pl.multiple_of(start, 8)
        ref[pl.ds(start, 8), :] = value

    def at7(t):
        return (t[0] * 7 + t[1]) * 7 + t[2]

    def at8(t):
        return (t[0] * 8 + t[1]) * 8 + t[2]

    def loop(count, body):
        def step(i, carry):
            body(i)
            return carry

        lax.fori_loop(0, count, step, 0)

    def line(lv, dim, v):
        q, half = lv.q, lv.half
        full = list(v) + [down(dim, v[0])]
        e = [full[j] + full[q - j] for j in range(half)]
        o = [full[j] - full[q - j] for j in range(half)]
        y = [None] * (q + 1)
        for i in range(half):
            ev, od = mix(lv.even[i], e), mix(lv.odd[i], o)
            y[i] = od if ev is None else ev + od
            y[q - i] = -od if ev is None else ev - od
        own = jnp.where(first[dim], float(lv.gain[q, q]), 0.0)
        y[0] = y[0] + up(dim, y[q]) + own * v[0]
        return y[:q]

    def partial_end(lv, v):
        return mix(lv.gain[lv.q, : lv.q], v)

    def lower_line(hi, lo, v):
        jmat = lagrange_matrix(gll_table(hi.q)[0], gll_table(lo.q)[0])
        r = jmat.T * hi.mass[None, :] / lo.mass[:, None]
        inner = range(1, hi.half)
        e = [v[n] + v[hi.q - n] for n in inner]
        o = [v[n] - v[hi.q - n] for n in inner]
        y = [None] * (lo.q + 1)
        for m in range(lo.half):
            ev = mix([0.5 * (r[m, n] + r[m, hi.q - n]) for n in inner], e)
            od = mix([0.5 * (r[m, n] - r[m, hi.q - n]) for n in inner], o)
            y[m], y[lo.q - m] = ev + od, ev - od
        y[0] = y[0] + float(r[0, 0]) * v[0]
        return y

    def raise_line(hi, lo, v):
        jmat = lagrange_matrix(gll_table(hi.q)[0], gll_table(lo.q)[0])
        e = [v[m] + v[lo.q - m] for m in range(lo.half)]
        o = [v[m] - v[lo.q - m] for m in range(lo.half)]
        y = [None] * (hi.q + 1)
        y[0] = v[0]
        for n in range(1, hi.half):
            ev = mix([0.5 * (jmat[n, m] + jmat[n, lo.q - m]) for m in range(lo.half)], e)
            od = mix([0.5 * (jmat[n, m] - jmat[n, lo.q - m]) for m in range(lo.half)], o)
            y[n], y[hi.q - n] = ev + od, ev - od
        return y[: hi.q]


    def store_face(name, dim, way, n, get):
        offset = SLOTS[(name, dim, way)][0]
        if dim == "c":
            acc = None
            for i in range(n):
                w = pack(dim, way, [get(i, k) for k in range(n)])
                acc = w if acc is None else jnp.where(lanes // 8 == i, spin(w, 0, 8 * i), acc)
            put(sbuf, offset, acc)
        else:
            for i in range(n):
                put(sbuf, offset + i, pack(dim, way, [get(i, k) for k in range(n)]))
        send((name, dim, way))

    def load_face(name, dim, way, n):
        offset = SLOTS[(name, dim, way)][0]
        receive((name, dim, way))
        if dim == "c":
            w = tile(rbuf, offset)
            return [[unpack(dim, way, spin(w, 0, -8 * i), k) for k in range(n)] for i in range(n)]
        return [
            [unpack(dim, way, tile(rbuf, offset + i), k) for k in range(n)] for i in range(n)
        ]

    def small_apply(lv, name, dv):
        n = lv.n
        for dim in ALL_DIMS:
            store_face(name, dim, -1, n, lambda i, k: dv[node(dim, 0, i, k)])
            store_face(
                name, dim, 1, n,
                lambda i, k: partial_end(lv, [dv[node(dim, m, i, k)] for m in range(n)]),
            )
        y = {}
        for dim in ALL_DIMS:
            for i in range(n):
                for k in range(n):
                    got = line(lv, dim, [dv[node(dim, m, i, k)] for m in range(n)])
                    for m in range(n):
                        t = node(dim, m, i, k)
                        y[t] = got[m] if t not in y else y[t] + got[m]
        drain(name)
        for dim in ALL_DIMS:
            before = load_face(name, dim, -1, n)
            after = load_face(name, dim, 1, n)
            for i in range(n):
                for k in range(n):
                    for m in range(n):
                        t = node(dim, m, i, k)
                        y[t] = y[t] + float(lv.gain[m, lv.q]) * before[i][k]
                    t = node(dim, 0, i, k)
                    y[t] = y[t] + after[i][k]
        return y

    def masked(t, v):
        if t[0] == 0:
            v = v * wall_a
        if t[1] == 0:
            v = v * wall_b
        return v

    def small_sum(lv, name, closed):
        n, q = lv.n, lv.q
        for dim in ALL_DIMS:
            for i in range(q + 1):
                for k in range(q + 1):
                    low, high = node(dim, 0, i, k), node(dim, q, i, k)
                    closed[low] = closed[low] + up(dim, closed[high])
        for dim in ALL_DIMS:
            store_face(name, dim, 1, n, lambda i, k: closed[node(dim, q, i, k)])
        for dims in SUBSETS[3:]:
            key = (name, dims, 1)
            for j, t in enumerate(plane(dims, n, q)):
                put(sbuf, SLOTS[key][0] + j, closed[t])
            send(key)
        drain(name)
        r = {t: closed[t] for t in itertools.product(range(n), repeat=3)}
        for dim in ALL_DIMS:
            got = load_face(name, dim, 1, n)
            for i in range(n):
                for k in range(n):
                    t = node(dim, 0, i, k)
                    r[t] = r[t] + got[i][k]
        for dims in SUBSETS[3:]:
            key = (name, dims, 1)
            receive(key)
            for j, t in enumerate(plane(dims, n, 0)):
                r[t] = r[t] + move(dims, 1, tile(rbuf, SLOTS[key][0] + j))
        return {t: masked(t, v) for t, v in r.items()}

    def plane(dims, n, end):
        ranges = [[end] if dim in dims else range(n) for dim in ALL_DIMS]
        return list(itertools.product(*ranges))

    def small_close(lv, name, v):
        n, q = lv.n, lv.q
        for dim in ALL_DIMS:
            store_face(name, dim, -1, n, lambda i, k: v[node(dim, 0, i, k)])
        for dims in SUBSETS[3:]:
            key = (name, dims, -1)
            for j, t in enumerate(plane(dims, n, 0)):
                put(sbuf, SLOTS[key][0] + j, v[t])
            send(key)
        drain(name)
        halo = {}
        for dim in ALL_DIMS:
            got = load_face(name, dim, -1, n)
            for i in range(n):
                for k in range(n):
                    halo[(dim, node(dim, q, i, k))] = got[i][k]
        for dims in SUBSETS[3:]:
            key = (name, dims, -1)
            receive(key)
            for j, t in enumerate(plane(dims, n, q)):
                halo[(dims, t)] = move(dims, -1, tile(rbuf, SLOTS[key][0] + j))
        return closure(lv, dict(v), halo)

    def closure(lv, field, halo):
        n, q = lv.n, lv.q

        def value(have, t):
            ends = "".join(dim for dim, i in zip(ALL_DIMS, t) if i == q and dim not in have)
            if not ends:
                return halo[(have, t)] if have else field[t]
            dim = ends[0]
            low = tuple(0 if d == dim else i for d, i in zip(ALL_DIMS, t))
            with_dim = "".join(d for d in ALL_DIMS if d in have or d == dim)
            return down(dim, value(have, low)) + value(with_dim, t)

        return {t: value("", t) for t in itertools.product(range(q + 1), repeat=3)}

    def first_step(lv, r):
        return {t: float(lv.inverse(*t) / lv.center) * v for t, v in r.items()}

    def next_step(lv, factor, dv, r):
        keep, gain = factor
        return {t: float(keep) * dv[t] + float(gain * lv.inverse(*t)) * r[t] for t in r}

    def subtract(r, y):
        return {t: masked(t, r[t] - y[t]) for t in r}

    def add(*fields):
        return {t: total(f[t] for f in fields) for t in fields[0]}

    def zero_block(i):
        rbuf[pl.ds(pl.multiple_of(i * 64, 64), 64), :] = jnp.zeros((64, 128), jnp.float32)

    loop(BUF_VREGS // 8, zero_block)

    for offset in BLOCKS:
        pl.semaphore_signal(
            pltpu.get_barrier_semaphore(),
            inc=1,
            device_id=device_at(*offset),
            device_id_type=pl.DeviceIdType.MESH,
        )

    def butterfly(vs):
        for bit in (1, 2, 4):
            new = list(vs)
            low = (lanes // bit) % 2 == 0
            for i in range(8):
                if not i & bit:
                    lo, hi = vs[i], vs[i + bit]
                    new[i] = jnp.where(low, lo, spin(hi, 0, bit))
                    new[i + bit] = jnp.where(low, spin(lo, 0, -bit), hi)
            vs = new
        return vs

    def enter(i):
        an, ael = lax.rem(i, 8), lax.div(i, 8)
        for b_hi in range(2):
            vs = [
                x[i, pl.ds((2 * b_hi + g % 2) * 8, 8), pl.ds((g // 2) * 128, 128)] for g in range(8)
            ]
            for cn, v in enumerate(butterfly(vs)):
                put(tr, (an * 8 + cn) * 8 + ael * 2 + b_hi, v)

    loop(32, enter)

    def by_nodes(an, bn, cn):
        return pl.ds((an * 8 + cn) * 64 + bn, 8, stride=8)

    def slab(a):
        v = {(b, c): tr[by_nodes(a, b, c), :] for b in range(8) for c in range(8)}
        for c in range(8):
            v[(0, c)] = v[(0, c)] + up("b", v[(7, c)])
        for b in range(8):
            v[(b, 0)] = v[(b, 0)] + up("c", v[(b, 7)])
        for (b, c), value in v.items():
            put(u, at8((a, b, c)), value)

    loop(8, slab)

    def join(b):
        for c in range(8):
            t = at8((0, b, c))
            put(u, t, tile(u, t) + up("a", tile(u, at8((7, b, c)))))

    loop(8, join)

    pl.semaphore_wait(pltpu.get_barrier_semaphore(), len(BLOCKS))

    def fine_face(name, dim, way, get):
        offset = SLOTS[(name, dim, way)][0]

        def row(i):
            vs = [get(i, k) for k in range(7)]
            if dim == "c":
                put(pk, i, pack(dim, way, vs))
            else:
                put(sbuf, offset + 2 * i, pack(dim, way, vs[:4]))
                put(sbuf, offset + 2 * i + 1, pack(dim, way, vs[4:]))

        loop(7, row)
        if dim == "c":
            acc = tile(pk, 0)
            for i in range(1, 7):
                acc = jnp.where(lanes // 16 == i, spin(tile(pk, i), 0, 16 * i), acc)
            put(sbuf, offset, acc)
        send((name, dim, way))

    def spread_c(name, way, base):
        w = tile(rbuf, SLOTS[(name, "c", way)][0])
        for i in range(7):
            put(pk, base + i, spin(w, 0, -16 * i))

    def fine_row(name, dim, way, i, base):
        if dim == "c":
            w = tile(pk, base + i)
            return [unpack(dim, way, w, k) for k in range(7)]
        offset = SLOTS[(name, dim, way)][0]
        lo, hi = tile(rbuf, offset + 2 * i), tile(rbuf, offset + 2 * i + 1)
        return [unpack(dim, way, lo if k < 4 else hi, k % 4) for k in range(7)]

    for dim in ALL_DIMS:
        fine_face("S7", dim, 1, lambda i, k: tile(u, at8(node(dim, 7, i, k))))
    for dims in SUBSETS[3:]:
        key = ("S7", dims, 1)
        for j, t in enumerate(plane(dims, 7, 7)):
            put(sbuf, SLOTS[key][0] + j, tile(u, at8(t)))
        send(key)
    for dim in ALL_DIMS:
        receive(("S7", dim, 1))
        if dim == "c":
            spread_c("S7", 1, 0)

        def add_face(i):
            got = fine_row("S7", dim, 1, i, 0)
            for k in range(7):
                t = at8(node(dim, 0, i, k))
                put(u, t, tile(u, t) + got[k])

        loop(7, add_face)
    for dims in SUBSETS[3:]:
        key = ("S7", dims, 1)
        receive(key)
        for j, t in enumerate(plane(dims, 7, 0)):
            put(u, at8(t), tile(u, at8(t)) + move(dims, 1, tile(rbuf, SLOTS[key][0] + j)))

    def first_fine(a):
        wall = jnp.where(a == 0, wall_a, 1.0)
        for b in range(7):
            for c in range(7):
                scale = tab[a * TAB + 16 + combo(b, c)]
                r = tile(u, at8((a, b, c))) * scale * wall
                if b == 0:
                    r = r * wall_b
                put(rho, at7((a, b, c)), r)
                put(d, at7((a, b, c)), (tab[a * TAB + combo(b, c)] * (1.0 / FINE.center)) * r)

    loop(7, first_fine)

    def fine_apply(name, after):
        for dim in ALL_DIMS:
            fine_face(name, dim, -1, lambda i, k: tile(d, at7(node(dim, 0, i, k))))
            fine_face(
                name, dim, 1,
                lambda i, k: partial_end(FINE, [tile(d, at7(node(dim, m, i, k))) for m in range(7)]),
            )

        def lines(dim, i):
            for k in range(7):
                at = [at7(node(dim, m, i, k)) for m in range(7)]
                got = line(FINE, dim, [tile(d, t) for t in at])
                for t, y in zip(at, got):
                    put(rho, t, tile(rho, t) - y)

        loop(7, lambda i: lines("a", i))

        def cross(i):
            lines("b", i)
            lines("c", i)

        loop(7, cross)

        drain(name)
        for dim in ALL_DIMS:
            for way in (1, -1):
                receive((name, dim, way))
        spread_c(name, 1, 0)
        spread_c(name, -1, 7)

        def side_a(i):
            got = fine_row(name, "a", -1, i, 0)
            add0 = fine_row(name, "a", 1, i, 0)
            for k in range(7):
                put(ha, i * 7 + k, got[k])
                t = at7((0, i, k))
                put(rho, t, tile(rho, t) - add0[k])

        loop(7, side_a)

        def finish(a):
            wall = jnp.where(a == 0, wall_a, 1.0)
            gain_a = tab[a * TAB + 32]
            b_before = fine_row(name, "b", -1, a, 0)
            b_after = fine_row(name, "b", 1, a, 0)
            c_before = fine_row(name, "c", -1, a, 7)
            c_after = fine_row(name, "c", 1, a, 0)
            for b in range(7):
                for c in range(7):
                    t = at7((a, b, c))
                    r = tile(rho, t) - gain_a * tile(ha, b * 7 + c)
                    r = r - float(FINE.gain[b, 7]) * b_before[c]
                    r = r - float(FINE.gain[c, 7]) * c_before[b]
                    if b == 0:
                        r = r - b_after[c]
                    if c == 0:
                        r = r - c_after[b]
                    r = r * wall
                    if b == 0:
                        r = r * wall_b
                    put(rho, t, r)
                    if after is not None:
                        after(a, b, c, r)

        loop(7, finish)

    fine_keep, fine_gain = FINE.factors(2)[0]

    def fine_next(a, b, c, r):
        t = at7((a, b, c))
        h = tab[a * TAB + combo(b, c)]
        return float(fine_keep) * tile(d, t) + (h * float(fine_gain)) * r

    def after_first(a, b, c, r):
        new = fine_next(a, b, c, r)
        t = at7((a, b, c))
        put(xs, at8((a, b, c)), tile(d, t) + new)
        put(d, t, new)

    def after_lift(a, b, c, r):
        t, s = at7((a, b, c)), at8((a, b, c))
        put(xs, s, tile(xs, s) + tile(d, t))
        put(d, t, (tab[a * TAB + combo(b, c)] * (1.0 / FINE.center)) * r)

    def after_post(a, b, c, r):
        t, s = at7((a, b, c)), at8((a, b, c))
        put(xs, s, tile(xs, s) + tile(d, t) + fine_next(a, b, c, r))

    fine_apply("f1", after_first)
    fine_apply("f2", None)

    def lower_a(b):
        for c in range(7):
            got = lower_line(FINE, MID, [tile(rho, at7((m, b, c))) for m in range(7)])
            for m in range(4):
                put(w1, (m * 7 + b) * 7 + c, got[m])

    loop(7, lower_a)

    def lower_b(a):
        for c in range(7):
            got = lower_line(FINE, MID, [tile(w1, (a * 7 + m) * 7 + c) for m in range(7)])
            for m in range(4):
                put(w2, (a * 4 + m) * 7 + c, got[m])

    loop(4, lower_b)
    closed = {}
    for a in range(4):
        for b in range(4):
            got = lower_line(FINE, MID, [tile(w2, (a * 4 + b) * 7 + m) for m in range(7)])
            for m in range(4):
                closed[(a, b, m)] = got[m]
    r3 = small_sum(MID, "S3", closed)

    mid_factor = MID.factors(2)[0]
    d3 = first_step(MID, r3)
    r3 = subtract(r3, small_apply(MID, "m1", d3))
    e3 = next_step(MID, mid_factor, d3, r3)
    x3 = add(d3, e3)
    r3 = subtract(r3, small_apply(MID, "m2", e3))

    closed = r3
    for dim in ALL_DIMS:
        new = {}
        others = sorted({tuple(i for dd, i in zip(ALL_DIMS, t) if dd != dim) for t in closed})
        for i, k in others:
            got = lower_line(MID, LOW, [closed[node(dim, m, i, k)] for m in range(3)])
            for m in range(2):
                new[node(dim, m, i, k)] = got[m]
        closed = new
    r1 = small_sum(LOW, "S1", closed)
    here = (0, 0, 0)
    origin = SLOTS[BLOCKS[0]][0]
    put(sbuf, origin, r1[here])

    def block_copy(offset):
        place, _, index = SLOTS[offset]
        src, dst = sbuf.at[pl.ds(origin * 8, 8)], rbuf.at[pl.ds(place * 8, 8)]
        return remote(src, dst, index, device_at(*offset))

    for offset in BLOCKS:
        block_copy(offset).start()
    drain()
    r = {here: r1[here]}
    for offset in BLOCKS:
        block_copy(offset).wait_recv()
        r[tuple(-o for o in offset)] = tile(rbuf, SLOTS[offset][0])

    def up_full(dim, v, before):
        if dim == "a":
            return spin(jnp.where(last["a"], before, v), 2, 0)
        if dim == "b":
            w = jnp.where(odd_lane, jnp.where(odd_row, spin(v, 1, 0), spin(before, -1, 0)), v)
            return jnp.where(odd_lane, spin(w, 0, 1), spin(w, 0, -1))
        t = jnp.where(lanes < 8, spin(v, 0, 10), spin(v, 0, 8))
        return jnp.where(lanes < 2, spin(before, 0, 2), t)

    def down_full(dim, v, after):
        if dim == "a":
            return spin(jnp.where(first["a"], after, v), -2, 0)
        if dim == "b":
            w = jnp.where(odd_lane, v, jnp.where(odd_row, spin(after, 1, 0), spin(v, -1, 0)))
            return jnp.where(odd_lane, spin(w, 0, 1), spin(w, 0, -1))
        t = jnp.where(lanes >= 120, spin(v, 0, -10), spin(v, 0, -8))
        return jnp.where(lanes >= 126, spin(after, 0, -2), t)

    def beside(dim, o, step):
        return tuple(i + step if d == dim else i for d, i in zip(ALL_DIMS, o))

    def both_sides(dim, f, o):
        before, after = f.get(beside(dim, o, -1), f[o]), f.get(beside(dim, o, 1), f[o])
        return up_full(dim, f[o], before) + down_full(dim, f[o], after)

    walls_a, walls_b = {}, {}
    for step in (-1, 0, 1):
        at_a, at_b = lax.rem(gy + step + ny, ny) == 0, lax.rem(gz + step + nz, nz) == 0
        walls_a[step] = jnp.where(first["a"] & at_a, 0.0, 1.0).astype(jnp.float32)
        walls_b[step] = jnp.where(first["b"] & at_b, 0.0, 1.0).astype(jnp.float32)

    own_low = 3.0 * float(LOW.gain[0, 0] + LOW.gain[1, 1])
    side_low = float(LOW.gain[0, 1])
    inverse_low = float(LOW.inverse(0, 0, 0))
    dl = {o: (inverse_low / LOW.center) * v for o, v in r.items()}
    x1 = dict(dl)
    for keep, gain in LOW.factors(COARSE_STEPS):
        new = {}
        for o in r:
            sides = total(both_sides(dim, dl, o) for dim in ALL_DIMS)
            left = r[o] - (own_low * dl[o] + side_low * sides)
            new[o] = left * (walls_a[o[0]] * walls_b[o[1]])
        r = new
        dl = {o: float(keep) * dl[o] + float(gain * inverse_low) * r[o] for o in r}
        x1 = add(x1, dl)

    def corners(f, dims):
        for dim in dims:
            new = {}
            for o, v in f.items():
                new[o] = v if o[ALL_DIMS.index(dim)] == 0 else None
            for o in f:
                if new[o] is None:
                    low = beside(dim, o, -1)
                    new[o] = down_full(dim, f[low], f[o])
            f = new
        return f

    def lift_low(f, dims):
        for dim in dims:
            new = {}
            rest = sorted({tuple(i for d, i in zip(ALL_DIMS, t) if d != dim) for t in f})
            for i, k in rest:
                got = raise_line(MID, LOW, [f[node(dim, m, i, k)] for m in range(2)])
                for m in range(3):
                    new[node(dim, m, i, k)] = got[m]
            f = new
        return f

    ends = list(itertools.product((0, 1), repeat=3))
    c3 = lift_low(corners({o: x1[o] for o in ends}, ALL_DIMS), "cba")
    y = {t: None for t in c3}
    for dim in ALL_DIMS:
        at = ALL_DIMS.index(dim)
        rest = ALL_DIMS.replace(dim, "")
        f = {}
        for o in ends:
            if o[at] == 0:
                f[o] = (x1[o] - 0.5 * both_sides(dim, x1, o)) * float(1.0 / MID.mass[0])
        for t, v in lift_low(corners(f, rest), rest).items():
            y[t] = v if y[t] is None else y[t] + v
    r3 = {t: masked(t, v if y[t] is None else v - y[t]) for t, v in r3.items()}
    d3 = first_step(MID, r3)
    r3 = subtract(r3, small_apply(MID, "m4", d3))
    e3 = next_step(MID, mid_factor, d3, r3)
    t3 = small_close(MID, "C3", add(x3, c3, d3, e3))

    for a in range(4):
        for b in range(4):
            got = raise_line(FINE, MID, [t3[(a, b, m)] for m in range(4)])
            for m in range(7):
                put(w2, (a * 4 + b) * 7 + m, got[m])

    def raise_b(a):
        for c in range(7):
            got = raise_line(FINE, MID, [tile(w2, (a * 4 + m) * 7 + c) for m in range(4)])
            for m in range(7):
                put(w1, (a * 7 + m) * 7 + c, got[m])

    loop(4, raise_b)

    def raise_a(b):
        for c in range(7):
            got = raise_line(FINE, MID, [tile(w1, (m * 7 + b) * 7 + c) for m in range(4)])
            for m in range(7):
                put(d, at7((m, b, c)), got[m])

    loop(7, raise_a)
    fine_apply("f3", after_lift)
    fine_apply("f4", after_post)

    for dim in ALL_DIMS:
        fine_face("C7", dim, -1, lambda i, k: tile(xs, at8(node(dim, 0, i, k))))
    for dims in SUBSETS[3:]:
        key = ("C7", dims, -1)
        for j, t in enumerate(plane(dims, 7, 0)):
            put(sbuf, SLOTS[key][0] + j, tile(xs, at8(t)))
        send(key)
    for dims in SUBSETS:
        receive(("C7", dims, -1))
    spread_c("C7", -1, 0)

    def edge(dims, j):
        return move(dims, -1, tile(rbuf, SLOTS[("C7", dims, -1)][0] + j))

    for dim in ALL_DIMS:

        def end_face(i):
            got = fine_row("C7", dim, -1, i, 0)
            for k in range(7):
                value = down(dim, tile(xs, at8(node(dim, 0, i, k)))) + got[k]
                put(xs, at8(node(dim, 7, i, k)), value)

        loop(7, end_face)

    hb = fine_row("C7", "b", -1, 0, 0)
    hc_a = fine_row("C7", "c", -1, 0, 0)
    hc_b = [fine_row("C7", "c", -1, i, 0)[0] for i in range(7)]
    for k in range(7):
        value = down("b", tile(xs, at8((7, 0, k)))) + down("a", hb[k]) + edge("ab", k)
        put(xs, at8((7, 7, k)), value)
        value = down("c", tile(xs, at8((7, k, 0)))) + down("a", hc_a[k]) + edge("ac", k)
        put(xs, at8((7, k, 7)), value)
        value = down("c", tile(xs, at8((k, 7, 0)))) + down("b", hc_b[k]) + edge("bc", k)
        put(xs, at8((k, 7, 7)), value)
    value = down("c", tile(xs, at8((7, 7, 0)))) + down("b", down("a", hc_a[0]))
    value = value + down("b", edge("ac", 0)) + down("a", edge("bc", 0)) + edge("abc", 0)
    put(xs, at8((7, 7, 7)), value)

    def leave_nodes(a):
        for b in range(8):
            for c in range(8):
                tr[by_nodes(a, b, c), :] = tile(xs, at8((a, b, c)))

    loop(8, leave_nodes)

    def leave(i):
        an, ael = lax.rem(i, 8), lax.div(i, 8)
        for b_hi in range(2):
            vs = butterfly([tile(tr, (an * 8 + cn) * 8 + ael * 2 + b_hi) for cn in range(8)])
            for g, v in enumerate(vs):
                out[i, pl.ds((2 * b_hi + g % 2) * 8, 8), pl.ds((g // 2) * 128, 128)] = v

    loop(32, leave)
    drain()
    for offset in BLOCKS:
        block_copy(offset).wait_send()


def solution(mesh):
    sizes = tuple(mesh.shape[axis] for axis in ("gx", "gy", "gz"))

    def body(*refs):
        kernel(sizes, *refs)

    def local(residual):
        vmem = lambda count: pltpu.VMEM((count * 8, 128), jnp.float32)
        return pl.pallas_call(
            body,
            out_shape=jax.ShapeDtypeStruct(residual.shape, jnp.float32),
            in_specs=[
                pl.BlockSpec(memory_space=pltpu.SMEM),
                pl.BlockSpec(memory_space=pltpu.VMEM),
            ],
            out_specs=pl.BlockSpec(memory_space=pltpu.VMEM),
            scratch_shapes=[
                vmem(512),
                vmem(512),
                vmem(343),
                vmem(343),
                vmem(512),
                vmem(196),
                vmem(112),
                vmem(49),
                vmem(16),
                vmem(BUF_VREGS),
                vmem(BUF_VREGS),
                pltpu.SemaphoreType.DMA((MESSAGES,)),
                pltpu.SemaphoreType.DMA((MESSAGES,)),
            ],
            compiler_params=pltpu.CompilerParams(
                collective_id=0, has_side_effects=True, vmem_limit_bytes=40 * 1024 * 1024
            ),
        )(jnp.asarray(table()), residual)

    return jax.shard_map(
        local,
        mesh=mesh,
        in_specs=(P("gy", "gz", "gx"),),
        out_specs=P("gy", "gz", "gx"),
        check_vma=False,
    )
```

time: 539 us -> 114 us (0.21); the launches traced: 533 us -> 114 us
  starting transfers between devices: 192 us -> 0 us
  waiting for transfers between devices: 166 us -> 0 us
  Pallas kernels: 0 us -> 111 us
  matrix products: 78.1 us -> 0 us
  local copies, waits for them, and re-layouts: 54.8 us -> 3.59 us
  other arithmetic: 39.3 us -> 0 us
    ppermute x72 -> x0, starting transfers between devices: 192 us -> none  [the longest x36 110 us: extended_2(): lax.ppermute(lax.slice_in_dim(block, 0, width, axis=dim), axis, backward)]
    ppermute x72 -> x0, waiting for transfers between devices: 166 us -> none  [the longest x36 119 us: extended_2(): lax.ppermute(lax.slice_in_dim(block, 0, width, axis=dim), axis, backward)]
    pallas_call x0 -> x1, Pallas kernels: none -> 111 us  [local(): pl.pallas_call(body, out_shape=jax.ShapeDtypeStruct(residual.shape, jnp.f...]
    dot_general x45 -> x0, matrix products: 78.1 us -> none  [the longest x15 23 us: pipe_apply(): jnp.einsum('abcj,ij->abci', vector.reshape(size_a, size_b, size_pipe // i...]
    add x34 -> x0, other arithmetic: 27.2 us -> none  [the longest x24 14.5 us: step_inner(): return middle + head_mask * preceding + tail_mask * following]
    another operation x8 -> x0, local copies, waits for them, and re-layouts: 17.3 us -> none  [the longest x3 7.76 us: pipe_apply(): vector.reshape(size_a, size_b, size_pipe // in_width, in_width)]
    reshape x14 -> x0, local copies, waits for them, and re-layouts: 15.1 us -> none  [the longest x6 7.57 us: local_stiffness(): along_b = jnp.einsum('abjc,Jj->abJc', vector.reshape(size_a, size_b // pe...]
    transpose x13 -> x0, local copies, waits for them, and re-layouts: 6.78 us -> none  [the longest x9 6.39 us: local_stiffness(): jnp.einsum('ajbc,Jj->aJbc', vector.reshape(size_a // per_elem, per_elem,...]
  transfers between devices with their start and end apart: 72 -> 0, of which waited for: 37 -> 0; matrix products, arithmetic and copies ran while one was open for 1% -> 0% of each run, Pallas kernels for 0% -> 0%
where the time goes in v1:
time: 114 us
  Pallas kernels  111 us (97%)
  local copies, waits for them, and re-layouts  3.59 us (3%)
    pallas_call x1, Pallas kernels, local(): pl.pallas_call(body, out_shape=jax.ShapeDtypeStruct(residual.shape, jnp.f...  111 us
    unnamed x5, local copies, waits for them, and re-layouts  3.59 us

profile of v1, /device:TPU:1, one launch (start us, length us, event | category | flops | bytes accessed | tf_op | source)
XLA Modules:
  0.0 114.3 jit_solution(1541672631543913910)
XLA Ops:
  0.0 0.0 copy-start
  0.0 1.6 %copy-done = f32[32,32,512]{2,1,0:T(8,128)S(1)} copy-done((f32[32,32,512]{2,1,0:T(8,128)S(1)}, f32[32,32,512]{2,1,0:T(8,128)}, u32[]{:S(2)}) %copy-start) | copy-done | bytes 2097176
  1.6 0.0 copy-start.1
  1.6 0.7 copy-done.1
  2.3 110.7 %shard_map.28 = f32[32,32,512]{2,1,0:T(8,128)S(1)} custom-call(f32[231]{0:T(256)S(1)} %copy-done.1, f32[32,32,512]{2,1,0:T(8,128)S(1)} %copy-done), custom_call_target="tpu_custom_call" | custom-call | tf_op jit(solution)/shard_map/pallas_call | solution.py:983
  112.9 1.3 %copy.4 = f32[32,32,512]{2,1,0:T(8,128)} copy(f32[32,32,512]{2,1,0:T(8,128)S(1)} %shard_map.28) | data formatting | bytes 4194304
Async XLA Ops:
  0.0 1.6 %copy-start = (f32[32,32,512]{2,1,0:T(8,128)S(1)}, f32[32,32,512]{2,1,0:T(8,128)}, u32[]{:S(2)}) copy-start(f32[32,32,512]{2,1,0:T(8,128)} %refs_1_.1) | copy-start | bytes 6291460
  1.6 0.7 copy-start.1

commit v2 on v1

--- a/solution.py
+++ b/solution.py
@@ -132,23 +132,7 @@
 FINE, MID, LOW = Level(ORDER), Level(MID_ORDER), Level(1)
 ALL_DIMS = "abc"
 SUBSETS = ("a", "b", "c", "ab", "ac", "bc", "abc")
-TAB = 33
 BLOCKS = [o for o in itertools.product((-1, 0, 1), repeat=3) if any(o)]
-
-
-def table():
-    rows = []
-    for a in range(7):
-        inverse = [FINE.inverse(a, b, c) for b in range(4) for c in range(4)]
-        scale = [
-            1.0 / (FINE.mass[a] * FINE.mass[b] * FINE.mass[c]) for b in range(4) for c in range(4)
-        ]
-        rows += inverse + scale + [FINE.gain[a, 7]]
-    return np.asarray(rows, np.float32)
-
-
-def combo(b, c):
-    return min(b, 7 - b) * 4 + min(c, 7 - c)
 
 
 def node(dim, m, i, k):
@@ -200,7 +184,7 @@
     )
 
 
-def kernel(sizes, tab, x, out, tr, u, rho, d, xs, w1, w2, ha, pk, sbuf, rbuf, ssem, rsem):
+def kernel(sizes, x, out, tr, u, rho, d, ya, yb, yc, xs, w1, w2, ha, pk, sbuf, rbuf, ssem, rsem):
     nx, ny, nz = sizes
     gx, gy, gz = lax.axis_index("gx"), lax.axis_index("gy"), lax.axis_index("gz")
     rows = lax.broadcasted_iota(jnp.int32, (8, 128), 0)
@@ -326,6 +310,35 @@
         if not isinstance(index, int):
             start = pl.multiple_of(start, 8)
         ref[pl.ds(start, 8), :] = value
+
+    def sub(ref, base, length):
+        start = base * 8
+        if not isinstance(base, int):
+            start = pl.multiple_of(start, 8)
+        return ref.at[pl.ds(start, length * 8)]
+
+    def line_view(ref, dim, i):
+        if dim == "a":
+            return sub(ref, i * 7, 301), lambda m, k: m * 49 + k
+        return sub(ref, i * 49, 49), (lambda m, k: m * 7 + k) if dim == "b" else (
+            lambda m, k: k * 7 + m
+        )
+
+    def by_class(i, values):
+        picked = jnp.where((i == 2) | (i == 5), values[2], values[3])
+        picked = jnp.where((i == 1) | (i == 6), values[1], picked)
+        return jnp.where(i == 0, values[0], picked)
+
+    def splat(value):
+        return jnp.full((8, 128), value, jnp.float32)
+
+    def inverse_slab(a):
+        alpha = splat(by_class(a, [float(v) for v in FINE.alpha[:4]]))
+        found = {}
+        for b in range(4):
+            for c in range(b, 4):
+                found[(b, c)] = 1.0 / (alpha + float(FINE.alpha[b] + FINE.alpha[c]))
+        return lambda b, c: found[tuple(sorted((min(b, 7 - b), min(c, 7 - c))))]
 
     def at7(t):
         return (t[0] * 7 + t[1]) * 7 + t[2]
@@ -551,57 +564,58 @@
             vs = new
         return vs
 
-    def enter(i):
-        an, ael = lax.rem(i, 8), lax.div(i, 8)
-        for b_hi in range(2):
-            vs = [
-                x[i, pl.ds((2 * b_hi + g % 2) * 8, 8), pl.ds((g // 2) * 128, 128)] for g in range(8)
-            ]
-            for cn, v in enumerate(butterfly(vs)):
-                put(tr, (an * 8 + cn) * 8 + ael * 2 + b_hi, v)
-
-    loop(32, enter)
-
-    def by_nodes(an, bn, cn):
-        return pl.ds((an * 8 + cn) * 64 + bn, 8, stride=8)
+    def enter(an):
+        to = sub(tr, an * 64, 64)
+        for ael in range(4):
+            for b_hi in range(2):
+                vs = [
+                    x[ael * 8 + an, pl.ds((2 * b_hi + g % 2) * 8, 8), pl.ds((g // 2) * 128, 128)]
+                    for g in range(8)
+                ]
+                for cn, v in enumerate(butterfly(vs)):
+                    put(to, cn * 8 + ael * 2 + b_hi, v)
+
+    loop(8, enter)
+
+    def by_nodes(bn, cn):
+        return pl.ds(cn * 64 + bn, 8, stride=8)
 
     def slab(a):
-        v = {(b, c): tr[by_nodes(a, b, c), :] for b in range(8) for c in range(8)}
+        at = sub(tr, a * 64, 64)
+        to = sub(u, a * 64, 64)
+        v = {(b, c): at[by_nodes(b, c), :] for b in range(8) for c in range(8)}
         for c in range(8):
             v[(0, c)] = v[(0, c)] + up("b", v[(7, c)])
         for b in range(8):
             v[(b, 0)] = v[(b, 0)] + up("c", v[(b, 7)])
         for (b, c), value in v.items():
-            put(u, at8((a, b, c)), value)
+            put(to, b * 8 + c, value)
 
     loop(8, slab)
 
-    def join(b):
+    for b in range(8):
         for c in range(8):
             t = at8((0, b, c))
             put(u, t, tile(u, t) + up("a", tile(u, at8((7, b, c)))))
 
-    loop(8, join)
-
     pl.semaphore_wait(pltpu.get_barrier_semaphore(), len(BLOCKS))
 
-    def fine_face(name, dim, way, get):
+    def face_row(name, dim, way, i, vs):
         offset = SLOTS[(name, dim, way)][0]
-
-        def row(i):
-            vs = [get(i, k) for k in range(7)]
-            if dim == "c":
-                put(pk, i, pack(dim, way, vs))
-            else:
-                put(sbuf, offset + 2 * i, pack(dim, way, vs[:4]))
-                put(sbuf, offset + 2 * i + 1, pack(dim, way, vs[4:]))
-
-        loop(7, row)
         if dim == "c":
-            acc = tile(pk, 0)
+            put(pk, i if way > 0 else i + 7, pack(dim, way, vs))
+        else:
+            to = sub(sbuf, offset + 2 * i, 2)
+            put(to, 0, pack(dim, way, vs[:4]))
+            put(to, 1, pack(dim, way, vs[4:]))
+
+    def send_face(name, dim, way):
+        if dim == "c":
+            base = 0 if way > 0 else 7
+            acc = tile(pk, base)
             for i in range(1, 7):
-                acc = jnp.where(lanes // 16 == i, spin(tile(pk, i), 0, 16 * i), acc)
-            put(sbuf, offset, acc)
+                acc = jnp.where(lanes // 16 == i, spin(tile(pk, base + i), 0, 16 * i), acc)
+            put(sbuf, SLOTS[(name, dim, way)][0], acc)
         send((name, dim, way))
 
     def spread_c(name, way, base):
@@ -614,151 +628,159 @@
             w = tile(pk, base + i)
             return [unpack(dim, way, w, k) for k in range(7)]
         offset = SLOTS[(name, dim, way)][0]
-        lo, hi = tile(rbuf, offset + 2 * i), tile(rbuf, offset + 2 * i + 1)
+        at = sub(rbuf, offset + 2 * i, 2)
+        lo, hi = tile(at, 0), tile(at, 1)
         return [unpack(dim, way, lo if k < 4 else hi, k % 4) for k in range(7)]
 
     for dim in ALL_DIMS:
-        fine_face("S7", dim, 1, lambda i, k: tile(u, at8(node(dim, 7, i, k))))
+        for i in range(7):
+            face_row("S7", dim, 1, i, [tile(u, at8(node(dim, 7, i, k))) for k in range(7)])
+        send_face("S7", dim, 1)
     for dims in SUBSETS[3:]:
         key = ("S7", dims, 1)
         for j, t in enumerate(plane(dims, 7, 7)):
             put(sbuf, SLOTS[key][0] + j, tile(u, at8(t)))
         send(key)
-    for dim in ALL_DIMS:
-        receive(("S7", dim, 1))
-        if dim == "c":
-            spread_c("S7", 1, 0)
-
-        def add_face(i):
-            got = fine_row("S7", dim, 1, i, 0)
-            for k in range(7):
-                t = at8(node(dim, 0, i, k))
-                put(u, t, tile(u, t) + got[k])
-
-        loop(7, add_face)
-    for dims in SUBSETS[3:]:
+    for dims in ("c", "b", "a", "bc", "ac", "ab", "abc"):
         key = ("S7", dims, 1)
         receive(key)
-        for j, t in enumerate(plane(dims, 7, 0)):
-            put(u, at8(t), tile(u, at8(t)) + move(dims, 1, tile(rbuf, SLOTS[key][0] + j)))
+        if dims == "c":
+            spread_c("S7", 1, 0)
+        elif dims == "a":
+            for i in range(7):
+                got = fine_row("S7", "a", 1, i, 0)
+                for k in range(7):
+                    t = at8((0, i, k))
+                    put(u, t, tile(u, t) + got[k])
+        elif len(dims) > 1:
+            for j, t in enumerate(plane(dims, 7, 0)):
+                put(u, at8(t), tile(u, at8(t)) + move(dims, 1, tile(rbuf, SLOTS[key][0] + j)))
 
     def first_fine(a):
         wall = jnp.where(a == 0, wall_a, 1.0)
+        from_u, to_rho, to_d = sub(u, a * 64, 64), sub(rho, a * 49, 49), sub(d, a * 49, 49)
+        mass_a = by_class(a, [float(1.0 / v) for v in FINE.mass[:4]])
+        inverse = inverse_slab(a)
+        b_after = fine_row("S7", "b", 1, a, 0)
+        c_after = fine_row("S7", "c", 1, a, 0)
         for b in range(7):
             for c in range(7):
-                scale = tab[a * TAB + 16 + combo(b, c)]
-                r = tile(u, at8((a, b, c))) * scale * wall
+                r = tile(from_u, b * 8 + c)
+                if b == 0:
+                    r = r + b_after[c]
+                if c == 0:
+                    r = r + c_after[b]
+                r = r * (float(1.0 / (FINE.mass[b] * FINE.mass[c])) * mass_a) * wall
                 if b == 0:
                     r = r * wall_b
-                put(rho, at7((a, b, c)), r)
-                put(d, at7((a, b, c)), (tab[a * TAB + combo(b, c)] * (1.0 / FINE.center)) * r)
+                put(to_rho, b * 7 + c, r)
+                put(to_d, b * 7 + c, (inverse(b, c) * float(1.0 / FINE.center)) * r)
 
     loop(7, first_fine)
 
     def fine_apply(name, after):
-        for dim in ALL_DIMS:
-            fine_face(name, dim, -1, lambda i, k: tile(d, at7(node(dim, 0, i, k))))
-            fine_face(
-                name, dim, 1,
-                lambda i, k: partial_end(FINE, [tile(d, at7(node(dim, m, i, k))) for m in range(7)]),
-            )
-
-        def lines(dim, i):
-            for k in range(7):
-                at = [at7(node(dim, m, i, k)) for m in range(7)]
-                got = line(FINE, dim, [tile(d, t) for t in at])
-                for t, y in zip(at, got):
-                    put(rho, t, tile(rho, t) - y)
-
-        loop(7, lambda i: lines("a", i))
-
-        def cross(i):
-            lines("b", i)
-            lines("c", i)
-
-        loop(7, cross)
+        for dims in ("a", "bc"):
+
+            def faces(i):
+                for dim in dims:
+                    at, place = line_view(d, dim, i)
+                    vs = [[tile(at, place(m, k)) for m in range(7)] for k in range(7)]
+                    face_row(name, dim, -1, i, [v[0] for v in vs])
+                    face_row(name, dim, 1, i, [partial_end(FINE, v) for v in vs])
+
+            loop(7, faces)
+            for dim in dims:
+                send_face(name, dim, -1)
+                send_face(name, dim, 1)
+
+        def lines(i):
+            for dim, y in zip(ALL_DIMS, (ya, yb, yc)):
+                at, place = line_view(d, dim, i)
+                to, _ = line_view(y, dim, i)
+                for k in range(7):
+                    got = line(FINE, dim, [tile(at, place(m, k)) for m in range(7)])
+                    for m in range(7):
+                        put(to, place(m, k), got[m])
+
+        loop(7, lines)
 
         drain(name)
-        for dim in ALL_DIMS:
+        for dim in "cba":
             for way in (1, -1):
                 receive((name, dim, way))
         spread_c(name, 1, 0)
         spread_c(name, -1, 7)
-
-        def side_a(i):
+        for i in range(7):
             got = fine_row(name, "a", -1, i, 0)
             add0 = fine_row(name, "a", 1, i, 0)
             for k in range(7):
                 put(ha, i * 7 + k, got[k])
                 t = at7((0, i, k))
-                put(rho, t, tile(rho, t) - add0[k])
-
-        loop(7, side_a)
+                put(ya, t, tile(ya, t) + add0[k])
 
         def finish(a):
             wall = jnp.where(a == 0, wall_a, 1.0)
-            gain_a = tab[a * TAB + 32]
+            gain_a = float(FINE.gain[6, 7])
+            for m in range(6):
+                gain_a = jnp.where(a == m, float(FINE.gain[m, 7]), gain_a)
+            gain_a = splat(gain_a)
+            inverse = inverse_slab(a)
             b_before = fine_row(name, "b", -1, a, 0)
             b_after = fine_row(name, "b", 1, a, 0)
             c_before = fine_row(name, "c", -1, a, 7)
             c_after = fine_row(name, "c", 1, a, 0)
+            at_rho, at_d, at_x = sub(rho, a * 49, 49), sub(d, a * 49, 49), sub(xs, a * 64, 64)
+            at_y = [sub(y, a * 49, 49) for y in (ya, yb, yc)]
             for b in range(7):
                 for c in range(7):
-                    t = at7((a, b, c))
-                    r = tile(rho, t) - gain_a * tile(ha, b * 7 + c)
-                    r = r - float(FINE.gain[b, 7]) * b_before[c]
-                    r = r - float(FINE.gain[c, 7]) * c_before[b]
+                    t, t8 = b * 7 + c, b * 8 + c
+                    y = total(tile(part, t) for part in at_y) + gain_a * tile(ha, t)
+                    y = y + float(FINE.gain[b, 7]) * b_before[c]
+                    y = y + float(FINE.gain[c, 7]) * c_before[b]
                     if b == 0:
-                        r = r - b_after[c]
+                        y = y + b_after[c]
                     if c == 0:
-                        r = r - c_after[b]
-                    r = r * wall
+                        y = y + c_after[b]
+                    r = (tile(at_rho, t) - y) * wall
                     if b == 0:
                         r = r * wall_b
-                    put(rho, t, r)
-                    if after is not None:
-                        after(a, b, c, r)
+                    put(at_rho, t, r)
+                    if after is None:
+                        continue
+                    old = tile(at_d, t)
+                    if after == "lift":
+                        put(at_x, t8, tile(at_x, t8) + old)
+                        put(at_d, t, (inverse(b, c) * float(1.0 / FINE.center)) * r)
+                        continue
+                    new = float(fine_keep) * old + (inverse(b, c) * float(fine_gain)) * r
+                    if after == "first":
+                        put(at_x, t8, old + new)
+                        put(at_d, t, new)
+                    else:
+                        put(at_x, t8, tile(at_x, t8) + old + new)
 
         loop(7, finish)
 
     fine_keep, fine_gain = FINE.factors(2)[0]
-
-    def fine_next(a, b, c, r):
-        t = at7((a, b, c))
-        h = tab[a * TAB + combo(b, c)]
-        return float(fine_keep) * tile(d, t) + (h * float(fine_gain)) * r
-
-    def after_first(a, b, c, r):
-        new = fine_next(a, b, c, r)
-        t = at7((a, b, c))
-        put(xs, at8((a, b, c)), tile(d, t) + new)
-        put(d, t, new)
-
-    def after_lift(a, b, c, r):
-        t, s = at7((a, b, c)), at8((a, b, c))
-        put(xs, s, tile(xs, s) + tile(d, t))
-        put(d, t, (tab[a * TAB + combo(b, c)] * (1.0 / FINE.center)) * r)
-
-    def after_post(a, b, c, r):
-        t, s = at7((a, b, c)), at8((a, b, c))
-        put(xs, s, tile(xs, s) + tile(d, t) + fine_next(a, b, c, r))
-
-    fine_apply("f1", after_first)
+    fine_apply("f1", "first")
     fine_apply("f2", None)
 
     def lower_a(b):
+        at, place = line_view(rho, "a", b)
+        to = sub(w1, b * 7, 154)
         for c in range(7):
-            got = lower_line(FINE, MID, [tile(rho, at7((m, b, c))) for m in range(7)])
+            got = lower_line(FINE, MID, [tile(at, place(m, c)) for m in range(7)])
             for m in range(4):
-                put(w1, (m * 7 + b) * 7 + c, got[m])
+                put(to, m * 49 + c, got[m])
 
     loop(7, lower_a)
 
     def lower_b(a):
+        at, to = sub(w1, a * 49, 49), sub(w2, a * 28, 28)
         for c in range(7):
-            got = lower_line(FINE, MID, [tile(w1, (a * 7 + m) * 7 + c) for m in range(7)])
+            got = lower_line(FINE, MID, [tile(at, m * 7 + c) for m in range(7)])
             for m in range(4):
-                put(w2, (a * 4 + m) * 7 + c, got[m])
+                put(to, m * 7 + c, got[m])
 
     loop(4, lower_b)
     closed = {}
@@ -897,25 +919,30 @@
                 put(w2, (a * 4 + b) * 7 + m, got[m])
 
     def raise_b(a):
+        at, to = sub(w2, a * 28, 28), sub(w1, a * 49, 49)
         for c in range(7):
-            got = raise_line(FINE, MID, [tile(w2, (a * 4 + m) * 7 + c) for m in range(4)])
+            got = raise_line(FINE, MID, [tile(at, m * 7 + c) for m in range(4)])
             for m in range(7):
-                put(w1, (a * 7 + m) * 7 + c, got[m])
+                put(to, m * 7 + c, got[m])
 
     loop(4, raise_b)
 
     def raise_a(b):
+        at = sub(w1, b * 7, 154)
+        to, place = line_view(d, "a", b)
         for c in range(7):
-            got = raise_line(FINE, MID, [tile(w1, (m * 7 + b) * 7 + c) for m in range(4)])
+            got = raise_line(FINE, MID, [tile(at, m * 49 + c) for m in range(4)])
             for m in range(7):
-                put(d, at7((m, b, c)), got[m])
+                put(to, place(m, c), got[m])
 
     loop(7, raise_a)
-    fine_apply("f3", after_lift)
-    fine_apply("f4", after_post)
+    fine_apply("f3", "lift")
+    fine_apply("f4", "post")
 
     for dim in ALL_DIMS:
-        fine_face("C7", dim, -1, lambda i, k: tile(xs, at8(node(dim, 0, i, k))))
+        for i in range(7):
+            face_row("C7", dim, -1, i, [tile(xs, at8(node(dim, 0, i, k))) for k in range(7)])
+        send_face("C7", dim, -1)
     for dims in SUBSETS[3:]:
         key = ("C7", dims, -1)
         for j, t in enumerate(plane(dims, 7, 0)):
@@ -929,14 +956,11 @@
         return move(dims, -1, tile(rbuf, SLOTS[("C7", dims, -1)][0] + j))
 
     for dim in ALL_DIMS:
-
-        def end_face(i):
+        for i in range(7):
             got = fine_row("C7", dim, -1, i, 0)
             for k in range(7):
                 value = down(dim, tile(xs, at8(node(dim, 0, i, k)))) + got[k]
                 put(xs, at8(node(dim, 7, i, k)), value)
-
-        loop(7, end_face)
 
     hb = fine_row("C7", "b", -1, 0, 0)
     hc_a = fine_row("C7", "c", -1, 0, 0)
@@ -953,20 +977,23 @@
     put(xs, at8((7, 7, 7)), value)
 
     def leave_nodes(a):
+        at, to = sub(xs, a * 64, 64), sub(tr, a * 64, 64)
         for b in range(8):
             for c in range(8):
-                tr[by_nodes(a, b, c), :] = tile(xs, at8((a, b, c)))
+                to[by_nodes(b, c), :] = tile(at, b * 8 + c)
 
     loop(8, leave_nodes)
 
-    def leave(i):
-        an, ael = lax.rem(i, 8), lax.div(i, 8)
-        for b_hi in range(2):
-            vs = butterfly([tile(tr, (an * 8 + cn) * 8 + ael * 2 + b_hi) for cn in range(8)])
-            for g, v in enumerate(vs):
-                out[i, pl.ds((2 * b_hi + g % 2) * 8, 8), pl.ds((g // 2) * 128, 128)] = v
-
-    loop(32, leave)
+    def leave(an):
+        at = sub(tr, an * 64, 64)
+        for ael in range(4):
+            for b_hi in range(2):
+                vs = butterfly([tile(at, cn * 8 + ael * 2 + b_hi) for cn in range(8)])
+                for g, v in enumerate(vs):
+                    b_at, c_at = pl.ds((2 * b_hi + g % 2) * 8, 8), pl.ds((g // 2) * 128, 128)
+                    out[ael * 8 + an, b_at, c_at] = v
+
+    loop(8, leave)
     drain()
     for offset in BLOCKS:
         block_copy(offset).wait_send()
@@ -984,13 +1011,15 @@
             body,
             out_shape=jax.ShapeDtypeStruct(residual.shape, jnp.float32),
             in_specs=[
-                pl.BlockSpec(memory_space=pltpu.SMEM),
                 pl.BlockSpec(memory_space=pltpu.VMEM),
             ],
             out_specs=pl.BlockSpec(memory_space=pltpu.VMEM),
             scratch_shapes=[
                 vmem(512),
                 vmem(512),
+                vmem(343),
+                vmem(343),
+                vmem(343),
                 vmem(343),
                 vmem(343),
                 vmem(512),
@@ -1006,7 +1035,7 @@
             compiler_params=pltpu.CompilerParams(
                 collective_id=0, has_side_effects=True, vmem_limit_bytes=40 * 1024 * 1024
             ),
-        )(jnp.asarray(table()), residual)
+        )(residual)
 
     return jax.shard_map(
         local,

time: 114 us -> 100 us (0.88)
  Pallas kernels: 111 us -> 97.2 us
    pallas_call x1, Pallas kernels: 111 us -> 97.2 us  [local(): pl.pallas_call(body, out_shape=jax.ShapeDtypeStruct(residual.shape, jnp.f...]
    unnamed x5 -> x3, local copies, waits for them, and re-layouts: 3.59 us -> 2.91 us
where the time goes in v2:
time: 100 us
  Pallas kernels  97.2 us (97%)
  local copies, waits for them, and re-layouts  2.91 us (3%)
    pallas_call x1, Pallas kernels, local(): pl.pallas_call(body, out_shape=jax.ShapeDtypeStruct(residual.shape, jnp.f...  97.2 us
    unnamed x3, local copies, waits for them, and re-layouts  2.91 us

profile of v2, /device:TPU:1, one launch (start us, length us, event | category | flops | bytes accessed | tf_op | source)
XLA Modules:
  0.0 100.1 jit_solution(10004367404744505484)
XLA Ops:
  0.0 0.0 copy-start
  0.0 1.6 %copy-done = f32[32,32,512]{2,1,0:T(8,128)S(1)} copy-done((f32[32,32,512]{2,1,0:T(8,128)S(1)}, f32[32,32,512]{2,1,0:T(8,128)}, u32[]{:S(2)}) %copy-start) | copy-done | bytes 2097176
  1.6 97.2 %shard_map.17 = f32[32,32,512]{2,1,0:T(8,128)S(1)} custom-call(f32[32,32,512]{2,1,0:T(8,128)S(1)} %copy-done), custom_call_target="tpu_custom_call" | custom-call | tf_op jit(solution)/shard_map/pallas_call | solution.py:1010
  98.8 1.3 %copy.3 = f32[32,32,512]{2,1,0:T(8,128)} copy(f32[32,32,512]{2,1,0:T(8,128)S(1)} %shard_map.17) | data formatting | bytes 4194304
Async XLA Ops:
  0.0 1.6 %copy-start = (f32[32,32,512]{2,1,0:T(8,128)S(1)}, f32[32,32,512]{2,1,0:T(8,128)}, u32[]{:S(2)}) copy-start(f32[32,32,512]{2,1,0:T(8,128)} %refs_0_.1) | copy-start | bytes 6291460

commit v3 on v2

--- a/solution.py
+++ b/solution.py
@@ -161,7 +161,7 @@
                 add((name, dim, way), face_vregs(n, dim))
     for name, n, way in (("S7", 7, 1), ("S3", 3, 1), ("S1", 1, 1), ("C3", 3, -1), ("C7", 7, -1)):
         for dims in SUBSETS:
-            add((name, dims, way), face_vregs(n, dims) if len(dims) == 1 else n ** (3 - len(dims)))
+            add((name, dims, way), face_vregs(n, dims) if len(dims) == 1 else 1)
     for offset in BLOCKS:
         add(offset, 1)
     return slots, -(-size // 8) * 8, count
@@ -184,7 +184,7 @@
     )
 
 
-def kernel(sizes, x, out, tr, u, rho, d, ya, yb, yc, xs, w1, w2, ha, pk, sbuf, rbuf, ssem, rsem):
+def kernel(sizes, x_hbm, out, x, tr, u, rho, d, ya, yb, yc, xs, w1, w2, ha, pk, sbuf, rbuf, ssem, rsem, xsem):
     nx, ny, nz = sizes
     gx, gy, gz = lax.axis_index("gx"), lax.axis_index("gy"), lax.axis_index("gz")
     rows = lax.broadcasted_iota(jnp.int32, (8, 128), 0)
@@ -254,11 +254,26 @@
         return jnp.where(mask, spin(v, way * row, way * lane), 0.0)
 
     def guarded(key, way, run):
-        name, dims, _ = key
-        if name in ("f1", "f2", "f3", "f4", "S7", "C7") and "a" in dims:
+        if "a" in key[1]:
             pl.when(gy < ny - 1 if way > 0 else gy > 0)(run)
         else:
             run()
+
+    def edge_spin(dims, way, v, j):
+        return spin(v, way * j, 0) if dims == "ab" else spin(v, 0, way * 2 * j)
+
+    def send_edge(name, dims, way, vs):
+        acc = total(edge_spin(dims, way, move(dims, way, v), j) for j, v in enumerate(vs))
+        put(sbuf, SLOTS[(name, dims, way)][0], acc)
+        send((name, dims, way))
+
+    def load_edge(name, dims, way, count):
+        w = tile(rbuf, SLOTS[(name, dims, way)][0])
+        mask = None
+        for dim in dims:
+            part = (first if way > 0 else last)[dim]
+            mask = part if mask is None else mask & part
+        return [jnp.where(mask, edge_spin(dims, -way, w, j), 0.0) for j in range(count)]
 
     def device_at(da, db, dc):
         return {
@@ -466,10 +481,7 @@
         for dim in ALL_DIMS:
             store_face(name, dim, 1, n, lambda i, k: closed[node(dim, q, i, k)])
         for dims in SUBSETS[3:]:
-            key = (name, dims, 1)
-            for j, t in enumerate(plane(dims, n, q)):
-                put(sbuf, SLOTS[key][0] + j, closed[t])
-            send(key)
+            send_edge(name, dims, 1, [closed[t] for t in plane(dims, n, q)])
         drain(name)
         r = {t: closed[t] for t in itertools.product(range(n), repeat=3)}
         for dim in ALL_DIMS:
@@ -479,10 +491,10 @@
                     t = node(dim, 0, i, k)
                     r[t] = r[t] + got[i][k]
         for dims in SUBSETS[3:]:
-            key = (name, dims, 1)
-            receive(key)
-            for j, t in enumerate(plane(dims, n, 0)):
-                r[t] = r[t] + move(dims, 1, tile(rbuf, SLOTS[key][0] + j))
+            receive((name, dims, 1))
+            places = plane(dims, n, 0)
+            for t, v in zip(places, load_edge(name, dims, 1, len(places))):
+                r[t] = r[t] + v
         return {t: masked(t, v) for t, v in r.items()}
 
     def plane(dims, n, end):
@@ -494,10 +506,7 @@
         for dim in ALL_DIMS:
             store_face(name, dim, -1, n, lambda i, k: v[node(dim, 0, i, k)])
         for dims in SUBSETS[3:]:
-            key = (name, dims, -1)
-            for j, t in enumerate(plane(dims, n, 0)):
-                put(sbuf, SLOTS[key][0] + j, v[t])
-            send(key)
+            send_edge(name, dims, -1, [v[t] for t in plane(dims, n, 0)])
         drain(name)
         halo = {}
         for dim in ALL_DIMS:
@@ -506,10 +515,10 @@
                 for k in range(n):
                     halo[(dim, node(dim, q, i, k))] = got[i][k]
         for dims in SUBSETS[3:]:
-            key = (name, dims, -1)
-            receive(key)
-            for j, t in enumerate(plane(dims, n, q)):
-                halo[(dims, t)] = move(dims, -1, tile(rbuf, SLOTS[key][0] + j))
+            receive((name, dims, -1))
+            places = plane(dims, n, q)
+            for t, got in zip(places, load_edge(name, dims, -1, len(places))):
+                halo[(dims, t)] = got
         return closure(lv, dict(v), halo)
 
     def closure(lv, field, halo):
@@ -538,6 +547,9 @@
 
     def add(*fields):
         return {t: total(f[t] for f in fields) for t in fields[0]}
+
+    for an in (7, 0, 1, 2, 3, 4, 5, 6):
+        pltpu.make_async_copy(x_hbm.at[:, an], x.at[:, an], xsem.at[an]).start()
 
     def zero_block(i):
         rbuf[pl.ds(pl.multiple_of(i * 64, 64), 64), :] = jnp.zeros((64, 128), jnp.float32)
@@ -569,13 +581,11 @@
         for ael in range(4):
             for b_hi in range(2):
                 vs = [
-                    x[ael * 8 + an, pl.ds((2 * b_hi + g % 2) * 8, 8), pl.ds((g // 2) * 128, 128)]
+                    x[ael, an, pl.ds((2 * b_hi + g % 2) * 8, 8), pl.ds((g // 2) * 128, 128)]
                     for g in range(8)
                 ]
                 for cn, v in enumerate(butterfly(vs)):
                     put(to, cn * 8 + ael * 2 + b_hi, v)
-
-    loop(8, enter)
 
     def by_nodes(bn, cn):
         return pl.ds(cn * 64 + bn, 8, stride=8)
@@ -591,14 +601,9 @@
         for (b, c), value in v.items():
             put(to, b * 8 + c, value)
 
-    loop(8, slab)
-
-    for b in range(8):
-        for c in range(8):
-            t = at8((0, b, c))
-            put(u, t, tile(u, t) + up("a", tile(u, at8((7, b, c)))))
-
-    pl.semaphore_wait(pltpu.get_barrier_semaphore(), len(BLOCKS))
+    fetch = [
+        pltpu.make_async_copy(x_hbm.at[:, an], x.at[:, an], xsem.at[an]) for an in range(8)
+    ]
 
     def face_row(name, dim, way, i, vs):
         offset = SLOTS[(name, dim, way)][0]
@@ -632,15 +637,31 @@
         lo, hi = tile(at, 0), tile(at, 1)
         return [unpack(dim, way, lo if k < 4 else hi, k % 4) for k in range(7)]
 
-    for dim in ALL_DIMS:
+    def start_sum(dims):
+        if len(dims) > 1:
+            send_edge("S7", dims, 1, [tile(u, at8(t)) for t in plane(dims, 7, 7)])
+            return
         for i in range(7):
-            face_row("S7", dim, 1, i, [tile(u, at8(node(dim, 7, i, k))) for k in range(7)])
-        send_face("S7", dim, 1)
-    for dims in SUBSETS[3:]:
-        key = ("S7", dims, 1)
-        for j, t in enumerate(plane(dims, 7, 7)):
-            put(sbuf, SLOTS[key][0] + j, tile(u, at8(t)))
-        send(key)
+            face_row("S7", dims, 1, i, [tile(u, at8(node(dims, 7, i, k))) for k in range(7)])
+        send_face("S7", dims, 1)
+
+    fetch[7].wait()
+    enter(7)
+    slab(7)
+    pl.semaphore_wait(pltpu.get_barrier_semaphore(), len(BLOCKS))
+    for dims in ("a", "ab", "ac", "abc"):
+        start_sum(dims)
+    for an in range(7):
+        fetch[an].wait()
+    loop(7, enter)
+    loop(7, slab)
+    for b in range(8):
+        for c in range(8):
+            t = at8((0, b, c))
+            put(u, t, tile(u, t) + up("a", tile(u, at8((7, b, c)))))
+    for dims in ("c", "b", "bc"):
+        start_sum(dims)
+
     for dims in ("c", "b", "a", "bc", "ac", "ab", "abc"):
         key = ("S7", dims, 1)
         receive(key)
@@ -653,8 +674,9 @@
                     t = at8((0, i, k))
                     put(u, t, tile(u, t) + got[k])
         elif len(dims) > 1:
-            for j, t in enumerate(plane(dims, 7, 0)):
-                put(u, at8(t), tile(u, at8(t)) + move(dims, 1, tile(rbuf, SLOTS[key][0] + j)))
+            places = plane(dims, 7, 0)
+            for t, v in zip(places, load_edge("S7", dims, 1, len(places))):
+                put(u, at8(t), tile(u, at8(t)) + v)
 
     def first_fine(a):
         wall = jnp.where(a == 0, wall_a, 1.0)
@@ -759,7 +781,19 @@
                     else:
                         put(at_x, t8, tile(at_x, t8) + old + new)
 
-        loop(7, finish)
+        finish(0)
+        if after == "post":
+            for dims in ("a", "ab", "ac", "abc"):
+                start_close(dims)
+        loop(6, lambda a: finish(a + 1))
+
+    def start_close(dims):
+        if len(dims) > 1:
+            send_edge("C7", dims, -1, [tile(xs, at8(t)) for t in plane(dims, 7, 0)])
+            return
+        for i in range(7):
+            face_row("C7", dims, -1, i, [tile(xs, at8(node(dims, 0, i, k))) for k in range(7)])
+        send_face("C7", dims, -1)
 
     fine_keep, fine_gain = FINE.factors(2)[0]
     fine_apply("f1", "first")
@@ -817,12 +851,24 @@
         src, dst = sbuf.at[pl.ds(origin * 8, 8)], rbuf.at[pl.ds(place * 8, 8)]
         return remote(src, dst, index, device_at(*offset))
 
-    for offset in BLOCKS:
-        block_copy(offset).start()
+    def block_copies(way, act):
+        for step in (1, 0, -1):
+            group = [o for o in BLOCKS if o[0] == step]
+
+            def run():
+                for offset in group:
+                    act(block_copy(offset))
+
+            if step:
+                pl.when(gy < ny - 1 if step * way > 0 else gy > 0)(run)
+            else:
+                run()
+
+    block_copies(1, lambda copy: copy.start())
     drain()
+    block_copies(-1, lambda copy: copy.wait_recv())
     r = {here: r1[here]}
     for offset in BLOCKS:
-        block_copy(offset).wait_recv()
         r[tuple(-o for o in offset)] = tile(rbuf, SLOTS[offset][0])
 
     def up_full(dim, v, before):
@@ -939,50 +985,14 @@
     fine_apply("f3", "lift")
     fine_apply("f4", "post")
 
-    for dim in ALL_DIMS:
-        for i in range(7):
-            face_row("C7", dim, -1, i, [tile(xs, at8(node(dim, 0, i, k))) for k in range(7)])
-        send_face("C7", dim, -1)
-    for dims in SUBSETS[3:]:
-        key = ("C7", dims, -1)
-        for j, t in enumerate(plane(dims, 7, 0)):
-            put(sbuf, SLOTS[key][0] + j, tile(xs, at8(t)))
-        send(key)
-    for dims in SUBSETS:
-        receive(("C7", dims, -1))
-    spread_c("C7", -1, 0)
-
-    def edge(dims, j):
-        return move(dims, -1, tile(rbuf, SLOTS[("C7", dims, -1)][0] + j))
-
-    for dim in ALL_DIMS:
-        for i in range(7):
-            got = fine_row("C7", dim, -1, i, 0)
-            for k in range(7):
-                value = down(dim, tile(xs, at8(node(dim, 0, i, k)))) + got[k]
-                put(xs, at8(node(dim, 7, i, k)), value)
-
-    hb = fine_row("C7", "b", -1, 0, 0)
-    hc_a = fine_row("C7", "c", -1, 0, 0)
-    hc_b = [fine_row("C7", "c", -1, i, 0)[0] for i in range(7)]
-    for k in range(7):
-        value = down("b", tile(xs, at8((7, 0, k)))) + down("a", hb[k]) + edge("ab", k)
-        put(xs, at8((7, 7, k)), value)
-        value = down("c", tile(xs, at8((7, k, 0)))) + down("a", hc_a[k]) + edge("ac", k)
-        put(xs, at8((7, k, 7)), value)
-        value = down("c", tile(xs, at8((k, 7, 0)))) + down("b", hc_b[k]) + edge("bc", k)
-        put(xs, at8((k, 7, 7)), value)
-    value = down("c", tile(xs, at8((7, 7, 0)))) + down("b", down("a", hc_a[0]))
-    value = value + down("b", edge("ac", 0)) + down("a", edge("bc", 0)) + edge("abc", 0)
-    put(xs, at8((7, 7, 7)), value)
+    for dims in ("b", "c", "bc"):
+        start_close(dims)
 
     def leave_nodes(a):
         at, to = sub(xs, a * 64, 64), sub(tr, a * 64, 64)
         for b in range(8):
             for c in range(8):
                 to[by_nodes(b, c), :] = tile(at, b * 8 + c)
-
-    loop(8, leave_nodes)
 
     def leave(an):
         at = sub(tr, an * 64, 64)
@@ -993,10 +1003,44 @@
                     b_at, c_at = pl.ds((2 * b_hi + g % 2) * 8, 8), pl.ds((g // 2) * 128, 128)
                     out[ael * 8 + an, b_at, c_at] = v
 
-    loop(8, leave)
+    def end_face(dim):
+        for i in range(7):
+            got = fine_row("C7", dim, -1, i, 0)
+            for k in range(7):
+                value = down(dim, tile(xs, at8(node(dim, 0, i, k)))) + got[k]
+                put(xs, at8(node(dim, 7, i, k)), value)
+
+    for dims in ("b", "c", "bc"):
+        receive(("C7", dims, -1))
+    spread_c("C7", -1, 0)
+    end_face("b")
+    end_face("c")
+    hb = fine_row("C7", "b", -1, 0, 0)
+    hc_a = fine_row("C7", "c", -1, 0, 0)
+    hc_b = [fine_row("C7", "c", -1, i, 0)[0] for i in range(7)]
+    edge_bc = load_edge("C7", "bc", -1, 7)
+    for k in range(7):
+        value = down("c", tile(xs, at8((k, 7, 0)))) + down("b", hc_b[k]) + edge_bc[k]
+        put(xs, at8((k, 7, 7)), value)
+    loop(7, leave_nodes)
+    loop(7, leave)
+
+    for dims in ("a", "ab", "ac", "abc"):
+        receive(("C7", dims, -1))
+    end_face("a")
+    edge_ab, edge_ac = load_edge("C7", "ab", -1, 7), load_edge("C7", "ac", -1, 7)
+    for k in range(7):
+        value = down("b", tile(xs, at8((7, 0, k)))) + down("a", hb[k]) + edge_ab[k]
+        put(xs, at8((7, 7, k)), value)
+        value = down("c", tile(xs, at8((7, k, 0)))) + down("a", hc_a[k]) + edge_ac[k]
+        put(xs, at8((7, k, 7)), value)
+    value = down("c", tile(xs, at8((7, 7, 0)))) + down("b", down("a", hc_a[0]))
+    value = value + down("b", edge_ac[0]) + down("a", edge_bc[0])
+    put(xs, at8((7, 7, 7)), value + load_edge("C7", "abc", -1, 1)[0])
+    leave_nodes(7)
+    leave(7)
     drain()
-    for offset in BLOCKS:
-        block_copy(offset).wait_send()
+    block_copies(1, lambda copy: copy.wait_send())
 
 
 def solution(mesh):
@@ -1011,10 +1055,11 @@
             body,
             out_shape=jax.ShapeDtypeStruct(residual.shape, jnp.float32),
             in_specs=[
-                pl.BlockSpec(memory_space=pltpu.VMEM),
+                pl.BlockSpec(memory_space=pl.ANY),
             ],
             out_specs=pl.BlockSpec(memory_space=pltpu.VMEM),
             scratch_shapes=[
+                pltpu.VMEM((4, 8, 32, 512), jnp.float32),
                 vmem(512),
                 vmem(512),
                 vmem(343),
@@ -1031,11 +1076,12 @@
                 vmem(BUF_VREGS),
                 pltpu.SemaphoreType.DMA((MESSAGES,)),
                 pltpu.SemaphoreType.DMA((MESSAGES,)),
+                pltpu.SemaphoreType.DMA((8,)),
             ],
             compiler_params=pltpu.CompilerParams(
                 collective_id=0, has_side_effects=True, vmem_limit_bytes=40 * 1024 * 1024
             ),
-        )(residual)
+        )(residual.reshape(4, 8, 32, 512))
 
     return jax.shard_map(
         local,

time: 100 us -> 97.7 us (0.977)
  Pallas kernels: 97.2 us -> 94.6 us
    pallas_call x1, Pallas kernels: 97.2 us -> 94.6 us  [local(): pl.pallas_call(body, out_shape=jax.ShapeDtypeStruct(residual.shape, jnp.f...]
where the time goes in v3:
time: 97.7 us; the launch traced here: 97.6 us
  Pallas kernels  94.6 us (97%)
  local copies, waits for them, and re-layouts  2.91 us (3%)
    pallas_call x1, Pallas kernels, local(): pl.pallas_call(body, out_shape=jax.ShapeDtypeStruct(residual.shape, jnp.f...  94.6 us
    unnamed x3, local copies, waits for them, and re-layouts  2.91 us

profile of v3, /device:TPU:1, one launch (start us, length us, event | category | flops | bytes accessed | tf_op | source)
XLA Modules:
  0.0 97.6 jit_solution(13797778871220405384)
XLA Ops:
  0.0 0.0 copy-start
  0.0 1.6 %copy-done = f32[32,32,512]{2,1,0:T(8,128)S(1)} copy-done((f32[32,32,512]{2,1,0:T(8,128)S(1)}, f32[32,32,512]{2,1,0:T(8,128)}, u32[]{:S(2)}) %copy-start) | copy-done | bytes 2097176
  1.6 94.6 %shard_map.17 = f32[32,32,512]{2,1,0:T(8,128)S(1)} custom-call(f32[4,8,32,512]{3,2,1,0:T(8,128)S(1)} %bitcast.1), custom_call_target="tpu_custom_call" | custom-call | tf_op jit(solution)/shard_map/pallas_call | solution.py:1054
  96.2 1.3 %copy.3 = f32[32,32,512]{2,1,0:T(8,128)} copy(f32[32,32,512]{2,1,0:T(8,128)S(1)} %shard_map.17) | data formatting | bytes 4194304
Async XLA Ops:
  0.0 1.6 %copy-start = (f32[32,32,512]{2,1,0:T(8,128)S(1)}, f32[32,32,512]{2,1,0:T(8,128)}, u32[]{:S(2)}) copy-start(f32[32,32,512]{2,1,0:T(8,128)} %param.1) | copy-start | bytes 6291460

commit v4 on v3

--- a/solution.py
+++ b/solution.py
@@ -292,10 +292,21 @@
             device_id_type=pl.DeviceIdType.MESH,
         )
 
+    turn = [0]
+
+    def slot(key):
+        name, dims, way = key
+        if name != "f":
+            return SLOTS[key]
+        offset, length, index = SLOTS[("f1", dims, way)]
+        shift = [SLOTS[("f2", dims, way)][i] - SLOTS[("f1", dims, way)][i] for i in (0, 2)]
+        return offset + turn[0] * shift[0], length, index + turn[0] * shift[1]
+
     def copy_of(key):
         name, dims, way = key
-        offset, length, index = SLOTS[key]
-        part = pl.ds(offset * 8, length * 8)
+        offset, length, index = slot(key)
+        start = offset * 8
+        part = pl.ds(start if isinstance(start, int) else pl.multiple_of(start, 8), length * 8)
         device = device_at(*(way if dim in dims else 0 for dim in ALL_DIMS))
         return remote(sbuf.at[part], rbuf.at[part], index, device)
 
@@ -303,7 +314,8 @@
 
     def send(key):
         guarded(key, key[2], lambda: copy_of(key).start())
-        pending.append(key)
+        if key[0] != "f":
+            pending.append(key)
 
     def receive(key):
         guarded(key, -key[2], lambda: copy_of(key).wait_recv())
@@ -452,7 +464,7 @@
                         t = node(dim, m, i, k)
                         y[t] = got[m] if t not in y else y[t] + got[m]
         drain(name)
-        for dim in ALL_DIMS:
+        for dim in "cba":
             before = load_face(name, dim, -1, n)
             after = load_face(name, dim, 1, n)
             for i in range(n):
@@ -484,13 +496,13 @@
             send_edge(name, dims, 1, [closed[t] for t in plane(dims, n, q)])
         drain(name)
         r = {t: closed[t] for t in itertools.product(range(n), repeat=3)}
-        for dim in ALL_DIMS:
+        for dim in "cba":
             got = load_face(name, dim, 1, n)
             for i in range(n):
                 for k in range(n):
                     t = node(dim, 0, i, k)
                     r[t] = r[t] + got[i][k]
-        for dims in SUBSETS[3:]:
+        for dims in ("bc", "ab", "ac", "abc"):
             receive((name, dims, 1))
             places = plane(dims, n, 0)
             for t, v in zip(places, load_edge(name, dims, 1, len(places))):
@@ -509,7 +521,7 @@
             send_edge(name, dims, -1, [v[t] for t in plane(dims, n, 0)])
         drain(name)
         halo = {}
-        for dim in ALL_DIMS:
+        for dim in "cba":
             got = load_face(name, dim, -1, n)
             for i in range(n):
                 for k in range(n):
@@ -606,7 +618,7 @@
     ]
 
     def face_row(name, dim, way, i, vs):
-        offset = SLOTS[(name, dim, way)][0]
+        offset = slot((name, dim, way))[0]
         if dim == "c":
             put(pk, i if way > 0 else i + 7, pack(dim, way, vs))
         else:
@@ -620,11 +632,11 @@
             acc = tile(pk, base)
             for i in range(1, 7):
                 acc = jnp.where(lanes // 16 == i, spin(tile(pk, base + i), 0, 16 * i), acc)
-            put(sbuf, SLOTS[(name, dim, way)][0], acc)
+            put(sbuf, slot((name, dim, way))[0], acc)
         send((name, dim, way))
 
     def spread_c(name, way, base):
-        w = tile(rbuf, SLOTS[(name, "c", way)][0])
+        w = tile(rbuf, slot((name, "c", way))[0])
         for i in range(7):
             put(pk, base + i, spin(w, 0, -16 * i))
 
@@ -632,7 +644,7 @@
         if dim == "c":
             w = tile(pk, base + i)
             return [unpack(dim, way, w, k) for k in range(7)]
-        offset = SLOTS[(name, dim, way)][0]
+        offset = slot((name, dim, way))[0]
         at = sub(rbuf, offset + 2 * i, 2)
         lo, hi = tile(at, 0), tile(at, 1)
         return [unpack(dim, way, lo if k < 4 else hi, k % 4) for k in range(7)]
@@ -681,6 +693,7 @@
     def first_fine(a):
         wall = jnp.where(a == 0, wall_a, 1.0)
         from_u, to_rho, to_d = sub(u, a * 64, 64), sub(rho, a * 49, 49), sub(d, a * 49, 49)
+        to_x = sub(xs, a * 64, 64)
         mass_a = by_class(a, [float(1.0 / v) for v in FINE.mass[:4]])
         inverse = inverse_slab(a)
         b_after = fine_row("S7", "b", 1, a, 0)
@@ -696,11 +709,16 @@
                 if b == 0:
                     r = r * wall_b
                 put(to_rho, b * 7 + c, r)
+                put(to_x, b * 8 + c, jnp.zeros((8, 128), jnp.float32))
                 put(to_d, b * 7 + c, (inverse(b, c) * float(1.0 / FINE.center)) * r)
 
     loop(7, first_fine)
-
-    def fine_apply(name, after):
+    drain()
+
+    def fine_apply(it):
+        name = "f"
+        turn[0] = it
+        ends = (it == 0) | (it == 3)
         for dims in ("a", "bc"):
 
             def faces(i):
@@ -726,7 +744,6 @@
 
         loop(7, lines)
 
-        drain(name)
         for dim in "cba":
             for way in (1, -1):
                 receive((name, dim, way))
@@ -747,6 +764,10 @@
                 gain_a = jnp.where(a == m, float(FINE.gain[m, 7]), gain_a)
             gain_a = splat(gain_a)
             inverse = inverse_slab(a)
+            keep = splat(jnp.where(ends, float(fine_keep), 0.0))
+            gain = splat(jnp.where(it == 2, float(1.0 / FINE.center), float(fine_gain)))
+            old_part = splat(jnp.where(it == 1, 0.0, 1.0))
+            new_part = splat(jnp.where(ends, 1.0, 0.0))
             b_before = fine_row(name, "b", -1, a, 0)
             b_after = fine_row(name, "b", 1, a, 0)
             c_before = fine_row(name, "c", -1, a, 7)
@@ -767,25 +788,24 @@
                     if b == 0:
                         r = r * wall_b
                     put(at_rho, t, r)
-                    if after is None:
-                        continue
                     old = tile(at_d, t)
-                    if after == "lift":
-                        put(at_x, t8, tile(at_x, t8) + old)
-                        put(at_d, t, (inverse(b, c) * float(1.0 / FINE.center)) * r)
-                        continue
-                    new = float(fine_keep) * old + (inverse(b, c) * float(fine_gain)) * r
-                    if after == "first":
-                        put(at_x, t8, old + new)
-                        put(at_d, t, new)
-                    else:
-                        put(at_x, t8, tile(at_x, t8) + old + new)
-
-        finish(0)
-        if after == "post":
-            for dims in ("a", "ab", "ac", "abc"):
-                start_close(dims)
-        loop(6, lambda a: finish(a + 1))
+                    new = keep * old + (inverse(b, c) * gain) * r
+                    put(at_x, t8, tile(at_x, t8) + (old_part * old + new_part * new))
+                    put(at_d, t, new)
+
+        def slab_end(a):
+            finish(a)
+
+            @pl.when((a == 0) & (it == 3))
+            def _():
+                for dims in ("a", "ab", "ac", "abc"):
+                    start_close(dims)
+
+        loop(7, slab_end)
+        for dim in ALL_DIMS:
+            for way in (1, -1):
+                key = (name, dim, way)
+                guarded(key, way, lambda: copy_of(key).wait_send())
 
     def start_close(dims):
         if len(dims) > 1:
@@ -796,194 +816,198 @@
         send_face("C7", dims, -1)
 
     fine_keep, fine_gain = FINE.factors(2)[0]
-    fine_apply("f1", "first")
-    fine_apply("f2", None)
-
-    def lower_a(b):
-        at, place = line_view(rho, "a", b)
-        to = sub(w1, b * 7, 154)
-        for c in range(7):
-            got = lower_line(FINE, MID, [tile(at, place(m, c)) for m in range(7)])
-            for m in range(4):
-                put(to, m * 49 + c, got[m])
-
-    loop(7, lower_a)
-
-    def lower_b(a):
-        at, to = sub(w1, a * 49, 49), sub(w2, a * 28, 28)
-        for c in range(7):
-            got = lower_line(FINE, MID, [tile(at, m * 7 + c) for m in range(7)])
-            for m in range(4):
-                put(to, m * 7 + c, got[m])
-
-    loop(4, lower_b)
-    closed = {}
-    for a in range(4):
-        for b in range(4):
-            got = lower_line(FINE, MID, [tile(w2, (a * 4 + b) * 7 + m) for m in range(7)])
-            for m in range(4):
-                closed[(a, b, m)] = got[m]
-    r3 = small_sum(MID, "S3", closed)
-
-    mid_factor = MID.factors(2)[0]
-    d3 = first_step(MID, r3)
-    r3 = subtract(r3, small_apply(MID, "m1", d3))
-    e3 = next_step(MID, mid_factor, d3, r3)
-    x3 = add(d3, e3)
-    r3 = subtract(r3, small_apply(MID, "m2", e3))
-
-    closed = r3
-    for dim in ALL_DIMS:
-        new = {}
-        others = sorted({tuple(i for dd, i in zip(ALL_DIMS, t) if dd != dim) for t in closed})
-        for i, k in others:
-            got = lower_line(MID, LOW, [closed[node(dim, m, i, k)] for m in range(3)])
-            for m in range(2):
-                new[node(dim, m, i, k)] = got[m]
-        closed = new
-    r1 = small_sum(LOW, "S1", closed)
-    here = (0, 0, 0)
-    origin = SLOTS[BLOCKS[0]][0]
-    put(sbuf, origin, r1[here])
-
-    def block_copy(offset):
-        place, _, index = SLOTS[offset]
-        src, dst = sbuf.at[pl.ds(origin * 8, 8)], rbuf.at[pl.ds(place * 8, 8)]
-        return remote(src, dst, index, device_at(*offset))
-
-    def block_copies(way, act):
-        for step in (1, 0, -1):
-            group = [o for o in BLOCKS if o[0] == step]
-
-            def run():
-                for offset in group:
-                    act(block_copy(offset))
-
-            if step:
-                pl.when(gy < ny - 1 if step * way > 0 else gy > 0)(run)
-            else:
-                run()
-
-    block_copies(1, lambda copy: copy.start())
-    drain()
-    block_copies(-1, lambda copy: copy.wait_recv())
-    r = {here: r1[here]}
-    for offset in BLOCKS:
-        r[tuple(-o for o in offset)] = tile(rbuf, SLOTS[offset][0])
-
-    def up_full(dim, v, before):
-        if dim == "a":
-            return spin(jnp.where(last["a"], before, v), 2, 0)
-        if dim == "b":
-            w = jnp.where(odd_lane, jnp.where(odd_row, spin(v, 1, 0), spin(before, -1, 0)), v)
-            return jnp.where(odd_lane, spin(w, 0, 1), spin(w, 0, -1))
-        t = jnp.where(lanes < 8, spin(v, 0, 10), spin(v, 0, 8))
-        return jnp.where(lanes < 2, spin(before, 0, 2), t)
-
-    def down_full(dim, v, after):
-        if dim == "a":
-            return spin(jnp.where(first["a"], after, v), -2, 0)
-        if dim == "b":
-            w = jnp.where(odd_lane, v, jnp.where(odd_row, spin(after, 1, 0), spin(v, -1, 0)))
-            return jnp.where(odd_lane, spin(w, 0, 1), spin(w, 0, -1))
-        t = jnp.where(lanes >= 120, spin(v, 0, -10), spin(v, 0, -8))
-        return jnp.where(lanes >= 126, spin(after, 0, -2), t)
-
-    def beside(dim, o, step):
-        return tuple(i + step if d == dim else i for d, i in zip(ALL_DIMS, o))
-
-    def both_sides(dim, f, o):
-        before, after = f.get(beside(dim, o, -1), f[o]), f.get(beside(dim, o, 1), f[o])
-        return up_full(dim, f[o], before) + down_full(dim, f[o], after)
-
-    walls_a, walls_b = {}, {}
-    for step in (-1, 0, 1):
-        at_a, at_b = lax.rem(gy + step + ny, ny) == 0, lax.rem(gz + step + nz, nz) == 0
-        walls_a[step] = jnp.where(first["a"] & at_a, 0.0, 1.0).astype(jnp.float32)
-        walls_b[step] = jnp.where(first["b"] & at_b, 0.0, 1.0).astype(jnp.float32)
-
-    own_low = 3.0 * float(LOW.gain[0, 0] + LOW.gain[1, 1])
-    side_low = float(LOW.gain[0, 1])
-    inverse_low = float(LOW.inverse(0, 0, 0))
-    dl = {o: (inverse_low / LOW.center) * v for o, v in r.items()}
-    x1 = dict(dl)
-    for keep, gain in LOW.factors(COARSE_STEPS):
-        new = {}
-        for o in r:
-            sides = total(both_sides(dim, dl, o) for dim in ALL_DIMS)
-            left = r[o] - (own_low * dl[o] + side_low * sides)
-            new[o] = left * (walls_a[o[0]] * walls_b[o[1]])
-        r = new
-        dl = {o: float(keep) * dl[o] + float(gain * inverse_low) * r[o] for o in r}
-        x1 = add(x1, dl)
-
-    def corners(f, dims):
-        for dim in dims:
+    def coarse():
+        def lower_a(b):
+            at, place = line_view(rho, "a", b)
+            to = sub(w1, b * 7, 154)
+            for c in range(7):
+                got = lower_line(FINE, MID, [tile(at, place(m, c)) for m in range(7)])
+                for m in range(4):
+                    put(to, m * 49 + c, got[m])
+
+        loop(7, lower_a)
+
+        def lower_b(a):
+            at, to = sub(w1, a * 49, 49), sub(w2, a * 28, 28)
+            for c in range(7):
+                got = lower_line(FINE, MID, [tile(at, m * 7 + c) for m in range(7)])
+                for m in range(4):
+                    put(to, m * 7 + c, got[m])
+
+        loop(4, lower_b)
+        closed = {}
+        for a in range(4):
+            for b in range(4):
+                got = lower_line(FINE, MID, [tile(w2, (a * 4 + b) * 7 + m) for m in range(7)])
+                for m in range(4):
+                    closed[(a, b, m)] = got[m]
+        r3 = small_sum(MID, "S3", closed)
+
+        mid_factor = MID.factors(2)[0]
+        d3 = first_step(MID, r3)
+        r3 = subtract(r3, small_apply(MID, "m1", d3))
+        e3 = next_step(MID, mid_factor, d3, r3)
+        x3 = add(d3, e3)
+        r3 = subtract(r3, small_apply(MID, "m2", e3))
+
+        closed = r3
+        for dim in ALL_DIMS:
             new = {}
-            for o, v in f.items():
-                new[o] = v if o[ALL_DIMS.index(dim)] == 0 else None
-            for o in f:
-                if new[o] is None:
-                    low = beside(dim, o, -1)
-                    new[o] = down_full(dim, f[low], f[o])
-            f = new
-        return f
-
-    def lift_low(f, dims):
-        for dim in dims:
+            others = sorted({tuple(i for dd, i in zip(ALL_DIMS, t) if dd != dim) for t in closed})
+            for i, k in others:
+                got = lower_line(MID, LOW, [closed[node(dim, m, i, k)] for m in range(3)])
+                for m in range(2):
+                    new[node(dim, m, i, k)] = got[m]
+            closed = new
+        r1 = small_sum(LOW, "S1", closed)
+        here = (0, 0, 0)
+        origin = SLOTS[BLOCKS[0]][0]
+        put(sbuf, origin, r1[here])
+
+        def block_copy(offset):
+            place, _, index = SLOTS[offset]
+            src, dst = sbuf.at[pl.ds(origin * 8, 8)], rbuf.at[pl.ds(place * 8, 8)]
+            return remote(src, dst, index, device_at(*offset))
+
+        def block_copies(way, act):
+            for step in (1, 0, -1):
+                group = [o for o in BLOCKS if o[0] == step]
+
+                def run():
+                    for offset in group:
+                        act(block_copy(offset))
+
+                if step:
+                    pl.when(gy < ny - 1 if step * way > 0 else gy > 0)(run)
+                else:
+                    run()
+
+        block_copies(1, lambda copy: copy.start())
+        drain()
+        block_copies(-1, lambda copy: copy.wait_recv())
+        r = {here: r1[here]}
+        for offset in BLOCKS:
+            r[tuple(-o for o in offset)] = tile(rbuf, SLOTS[offset][0])
+
+        def up_full(dim, v, before):
+            if dim == "a":
+                return spin(jnp.where(last["a"], before, v), 2, 0)
+            if dim == "b":
+                w = jnp.where(odd_lane, jnp.where(odd_row, spin(v, 1, 0), spin(before, -1, 0)), v)
+                return jnp.where(odd_lane, spin(w, 0, 1), spin(w, 0, -1))
+            t = jnp.where(lanes < 8, spin(v, 0, 10), spin(v, 0, 8))
+            return jnp.where(lanes < 2, spin(before, 0, 2), t)
+
+        def down_full(dim, v, after):
+            if dim == "a":
+                return spin(jnp.where(first["a"], after, v), -2, 0)
+            if dim == "b":
+                w = jnp.where(odd_lane, v, jnp.where(odd_row, spin(after, 1, 0), spin(v, -1, 0)))
+                return jnp.where(odd_lane, spin(w, 0, 1), spin(w, 0, -1))
+            t = jnp.where(lanes >= 120, spin(v, 0, -10), spin(v, 0, -8))
+            return jnp.where(lanes >= 126, spin(after, 0, -2), t)
+
+        def beside(dim, o, step):
+            return tuple(i + step if d == dim else i for d, i in zip(ALL_DIMS, o))
+
+        def both_sides(dim, f, o):
+            before, after = f.get(beside(dim, o, -1), f[o]), f.get(beside(dim, o, 1), f[o])
+            return up_full(dim, f[o], before) + down_full(dim, f[o], after)
+
+        walls_a, walls_b = {}, {}
+        for step in (-1, 0, 1):
+            at_a, at_b = lax.rem(gy + step + ny, ny) == 0, lax.rem(gz + step + nz, nz) == 0
+            walls_a[step] = jnp.where(first["a"] & at_a, 0.0, 1.0).astype(jnp.float32)
+            walls_b[step] = jnp.where(first["b"] & at_b, 0.0, 1.0).astype(jnp.float32)
+
+        own_low = 3.0 * float(LOW.gain[0, 0] + LOW.gain[1, 1])
+        side_low = float(LOW.gain[0, 1])
+        inverse_low = float(LOW.inverse(0, 0, 0))
+        dl = {o: (inverse_low / LOW.center) * v for o, v in r.items()}
+        x1 = dict(dl)
+        for keep, gain in LOW.factors(COARSE_STEPS):
             new = {}
-            rest = sorted({tuple(i for d, i in zip(ALL_DIMS, t) if d != dim) for t in f})
-            for i, k in rest:
-                got = raise_line(MID, LOW, [f[node(dim, m, i, k)] for m in range(2)])
-                for m in range(3):
-                    new[node(dim, m, i, k)] = got[m]
-            f = new
-        return f
-
-    ends = list(itertools.product((0, 1), repeat=3))
-    c3 = lift_low(corners({o: x1[o] for o in ends}, ALL_DIMS), "cba")
-    y = {t: None for t in c3}
-    for dim in ALL_DIMS:
-        at = ALL_DIMS.index(dim)
-        rest = ALL_DIMS.replace(dim, "")
-        f = {}
-        for o in ends:
-            if o[at] == 0:
-                f[o] = (x1[o] - 0.5 * both_sides(dim, x1, o)) * float(1.0 / MID.mass[0])
-        for t, v in lift_low(corners(f, rest), rest).items():
-            y[t] = v if y[t] is None else y[t] + v
-    r3 = {t: masked(t, v if y[t] is None else v - y[t]) for t, v in r3.items()}
-    d3 = first_step(MID, r3)
-    r3 = subtract(r3, small_apply(MID, "m4", d3))
-    e3 = next_step(MID, mid_factor, d3, r3)
-    t3 = small_close(MID, "C3", add(x3, c3, d3, e3))
-
-    for a in range(4):
-        for b in range(4):
-            got = raise_line(FINE, MID, [t3[(a, b, m)] for m in range(4)])
-            for m in range(7):
-                put(w2, (a * 4 + b) * 7 + m, got[m])
-
-    def raise_b(a):
-        at, to = sub(w2, a * 28, 28), sub(w1, a * 49, 49)
-        for c in range(7):
-            got = raise_line(FINE, MID, [tile(at, m * 7 + c) for m in range(4)])
-            for m in range(7):
-                put(to, m * 7 + c, got[m])
-
-    loop(4, raise_b)
-
-    def raise_a(b):
-        at = sub(w1, b * 7, 154)
-        to, place = line_view(d, "a", b)
-        for c in range(7):
-            got = raise_line(FINE, MID, [tile(at, m * 49 + c) for m in range(4)])
-            for m in range(7):
-                put(to, place(m, c), got[m])
-
-    loop(7, raise_a)
-    fine_apply("f3", "lift")
-    fine_apply("f4", "post")
+            for o in r:
+                sides = total(both_sides(dim, dl, o) for dim in ALL_DIMS)
+                left = r[o] - (own_low * dl[o] + side_low * sides)
+                new[o] = left * (walls_a[o[0]] * walls_b[o[1]])
+            r = new
+            dl = {o: float(keep) * dl[o] + float(gain * inverse_low) * r[o] for o in r}
+            x1 = add(x1, dl)
+
+        def corners(f, dims):
+            for dim in dims:
+                new = {}
+                for o, v in f.items():
+                    new[o] = v if o[ALL_DIMS.index(dim)] == 0 else None
+                for o in f:
+                    if new[o] is None:
+                        low = beside(dim, o, -1)
+                        new[o] = down_full(dim, f[low], f[o])
+                f = new
+            return f
+
+        def lift_low(f, dims):
+            for dim in dims:
+                new = {}
+                rest = sorted({tuple(i for d, i in zip(ALL_DIMS, t) if d != dim) for t in f})
+                for i, k in rest:
+                    got = raise_line(MID, LOW, [f[node(dim, m, i, k)] for m in range(2)])
+                    for m in range(3):
+                        new[node(dim, m, i, k)] = got[m]
+                f = new
+            return f
+
+        ends = list(itertools.product((0, 1), repeat=3))
+        c3 = lift_low(corners({o: x1[o] for o in ends}, ALL_DIMS), "cba")
+        y = {t: None for t in c3}
+        for dim in ALL_DIMS:
+            at = ALL_DIMS.index(dim)
+            rest = ALL_DIMS.replace(dim, "")
+            f = {}
+            for o in ends:
+                if o[at] == 0:
+                    f[o] = (x1[o] - 0.5 * both_sides(dim, x1, o)) * float(1.0 / MID.mass[0])
+            for t, v in lift_low(corners(f, rest), rest).items():
+                y[t] = v if y[t] is None else y[t] + v
+        r3 = {t: masked(t, v if y[t] is None else v - y[t]) for t, v in r3.items()}
+        d3 = first_step(MID, r3)
+        r3 = subtract(r3, small_apply(MID, "m4", d3))
+        e3 = next_step(MID, mid_factor, d3, r3)
+        t3 = small_close(MID, "C3", add(x3, c3, d3, e3))
+
+        for a in range(4):
+            for b in range(4):
+                got = raise_line(FINE, MID, [t3[(a, b, m)] for m in range(4)])
+                for m in range(7):
+                    put(w2, (a * 4 + b) * 7 + m, got[m])
+
+        def raise_b(a):
+            at, to = sub(w2, a * 28, 28), sub(w1, a * 49, 49)
+            for c in range(7):
+                got = raise_line(FINE, MID, [tile(at, m * 7 + c) for m in range(4)])
+                for m in range(7):
+                    put(to, m * 7 + c, got[m])
+
+        loop(4, raise_b)
+
+        def raise_a(b):
+            at = sub(w1, b * 7, 154)
+            to, place = line_view(d, "a", b)
+            for c in range(7):
+                got = raise_line(FINE, MID, [tile(at, m * 49 + c) for m in range(4)])
+                for m in range(7):
+                    put(to, place(m, c), got[m])
+
+        loop(7, raise_a)
+        drain()
+        block_copies(1, lambda copy: copy.wait_send())
+
+    def one_turn(it):
+        pl.when(it == 2)(coarse)
+        fine_apply(it)
+
+    loop(4, one_turn)
 
     for dims in ("b", "c", "bc"):
         start_close(dims)
@@ -1040,8 +1064,6 @@
     leave_nodes(7)
     leave(7)
     drain()
-    block_copies(1, lambda copy: copy.wait_send())
-
 
 def solution(mesh):
     sizes = tuple(mesh.shape[axis] for axis in ("gx", "gy", "gz"))

time: 97.7 us -> 99.4 us (1.017)
  Pallas kernels: 94.6 us -> 96.4 us
    pallas_call x1, Pallas kernels: 94.6 us -> 96.4 us  [local(): pl.pallas_call(body, out_shape=jax.ShapeDtypeStruct(residual.shape, jnp.f...]
where the time goes in v4:
time: 99.4 us; the launch traced here: 99.3 us
  Pallas kernels  96.4 us (97%)
  local copies, waits for them, and re-layouts  2.91 us (3%)
    pallas_call x1, Pallas kernels, local(): pl.pallas_call(body, out_shape=jax.ShapeDtypeStruct(residual.shape, jnp.f...  96.4 us
    unnamed x3, local copies, waits for them, and re-layouts  2.91 us

profile of v4, /device:TPU:1, one launch (start us, length us, event | category | flops | bytes accessed | tf_op | source)
XLA Modules:
  0.0 99.3 jit_solution(6615977982878742499)
XLA Ops:
  0.0 0.0 copy-start
  0.0 1.6 %copy-done = f32[32,32,512]{2,1,0:T(8,128)S(1)} copy-done((f32[32,32,512]{2,1,0:T(8,128)S(1)}, f32[32,32,512]{2,1,0:T(8,128)}, u32[]{:S(2)}) %copy-start) | copy-done | bytes 2097176
  1.6 96.4 %shard_map.17 = f32[32,32,512]{2,1,0:T(8,128)S(1)} custom-call(f32[4,8,32,512]{3,2,1,0:T(8,128)S(1)} %bitcast.1), custom_call_target="tpu_custom_call" | custom-call | tf_op jit(solution)/shard_map/pallas_call | solution.py:1076
  98.0 1.3 %copy.3 = f32[32,32,512]{2,1,0:T(8,128)} copy(f32[32,32,512]{2,1,0:T(8,128)S(1)} %shard_map.17) | data formatting | bytes 4194304
Async XLA Ops:
  0.0 1.6 %copy-start = (f32[32,32,512]{2,1,0:T(8,128)S(1)}, f32[32,32,512]{2,1,0:T(8,128)}, u32[]{:S(2)}) copy-start(f32[32,32,512]{2,1,0:T(8,128)} %param.1) | copy-start | bytes 6291460

commit v5 on v3

--- a/solution.py
+++ b/solution.py
@@ -184,7 +184,7 @@
     )
 
 
-def kernel(sizes, x_hbm, out, x, tr, u, rho, d, ya, yb, yc, xs, w1, w2, ha, pk, sbuf, rbuf, ssem, rsem, xsem):
+def kernel(sizes, x_hbm, out_hbm, x, out, tr, u, rho, d, ya, yb, yc, xs, w1, w2, ha, pk, sbuf, rbuf, ssem, rsem, xsem, osem):
     nx, ny, nz = sizes
     gx, gy, gz = lax.axis_index("gx"), lax.axis_index("gy"), lax.axis_index("gz")
     rows = lax.broadcasted_iota(jnp.int32, (8, 128), 0)
@@ -374,8 +374,9 @@
         e = [full[j] + full[q - j] for j in range(half)]
         o = [full[j] - full[q - j] for j in range(half)]
         y = [None] * (q + 1)
+        e = [v - e[0] for v in e[1:]]
         for i in range(half):
-            ev, od = mix(lv.even[i], e), mix(lv.odd[i], o)
+            ev, od = mix(lv.even[i][1:], e), mix(lv.odd[i], o)
             y[i] = od if ev is None else ev + od
             y[q - i] = -od if ev is None else ev - od
         own = jnp.where(first[dim], float(lv.gain[q, q]), 0.0)
@@ -452,7 +453,7 @@
                         t = node(dim, m, i, k)
                         y[t] = got[m] if t not in y else y[t] + got[m]
         drain(name)
-        for dim in ALL_DIMS:
+        for dim in "cba":
             before = load_face(name, dim, -1, n)
             after = load_face(name, dim, 1, n)
             for i in range(n):
@@ -484,13 +485,13 @@
             send_edge(name, dims, 1, [closed[t] for t in plane(dims, n, q)])
         drain(name)
         r = {t: closed[t] for t in itertools.product(range(n), repeat=3)}
-        for dim in ALL_DIMS:
+        for dim in "cba":
             got = load_face(name, dim, 1, n)
             for i in range(n):
                 for k in range(n):
                     t = node(dim, 0, i, k)
                     r[t] = r[t] + got[i][k]
-        for dims in SUBSETS[3:]:
+        for dims in ("bc", "ab", "ac", "abc"):
             receive((name, dims, 1))
             places = plane(dims, n, 0)
             for t, v in zip(places, load_edge(name, dims, 1, len(places))):
@@ -509,7 +510,7 @@
             send_edge(name, dims, -1, [v[t] for t in plane(dims, n, 0)])
         drain(name)
         halo = {}
-        for dim in ALL_DIMS:
+        for dim in "cba":
             got = load_face(name, dim, -1, n)
             for i in range(n):
                 for k in range(n):
@@ -1001,7 +1002,7 @@
                 vs = butterfly([tile(at, cn * 8 + ael * 2 + b_hi) for cn in range(8)])
                 for g, v in enumerate(vs):
                     b_at, c_at = pl.ds((2 * b_hi + g % 2) * 8, 8), pl.ds((g // 2) * 128, 128)
-                    out[ael * 8 + an, b_at, c_at] = v
+                    out[ael, an, b_at, c_at] = v
 
     def end_face(dim):
         for i in range(7):
@@ -1024,6 +1025,11 @@
         put(xs, at8((k, 7, 7)), value)
     loop(7, leave_nodes)
     loop(7, leave)
+    store = [
+        pltpu.make_async_copy(out.at[:, an], out_hbm.at[:, an], osem.at[an]) for an in range(8)
+    ]
+    for an in range(7):
+        store[an].start()
 
     for dims in ("a", "ab", "ac", "abc"):
         receive(("C7", dims, -1))
@@ -1039,6 +1045,9 @@
     put(xs, at8((7, 7, 7)), value + load_edge("C7", "abc", -1, 1)[0])
     leave_nodes(7)
     leave(7)
+    store[7].start()
+    for copy in store:
+        copy.wait()
     drain()
     block_copies(1, lambda copy: copy.wait_send())
 
@@ -1053,12 +1062,13 @@
         vmem = lambda count: pltpu.VMEM((count * 8, 128), jnp.float32)
         return pl.pallas_call(
             body,
-            out_shape=jax.ShapeDtypeStruct(residual.shape, jnp.float32),
+            out_shape=jax.ShapeDtypeStruct((4, 8, 32, 512), jnp.float32),
             in_specs=[
                 pl.BlockSpec(memory_space=pl.ANY),
             ],
-            out_specs=pl.BlockSpec(memory_space=pltpu.VMEM),
+            out_specs=pl.BlockSpec(memory_space=pl.ANY),
             scratch_shapes=[
+                pltpu.VMEM((4, 8, 32, 512), jnp.float32),
                 pltpu.VMEM((4, 8, 32, 512), jnp.float32),
                 vmem(512),
                 vmem(512),
@@ -1077,11 +1087,12 @@
                 pltpu.SemaphoreType.DMA((MESSAGES,)),
                 pltpu.SemaphoreType.DMA((MESSAGES,)),
                 pltpu.SemaphoreType.DMA((8,)),
+                pltpu.SemaphoreType.DMA((8,)),
             ],
             compiler_params=pltpu.CompilerParams(
-                collective_id=0, has_side_effects=True, vmem_limit_bytes=40 * 1024 * 1024
+                collective_id=0, has_side_effects=True, vmem_limit_bytes=60 * 1024 * 1024
             ),
-        )(residual.reshape(4, 8, 32, 512))
+        )(residual.reshape(4, 8, 32, 512)).reshape(residual.shape)
 
     return jax.shard_map(
         local,

time: 97.7 us -> 99.1 us (1.014)
  Pallas kernels: 94.6 us -> 95.7 us
    pallas_call x1, Pallas kernels: 94.6 us -> 95.7 us  [local(): pl.pallas_call(body, out_shape=jax.ShapeDtypeStruct((4, 8, 32, 512), jnp....]
    unnamed x3 -> x1, local copies, waits for them, and re-layouts: 2.91 us -> 3.19 us
where the time goes in v5:
time: 99.1 us; the launch traced here: 98.9 us
  Pallas kernels  95.7 us (97%)
  local copies, waits for them, and re-layouts  3.19 us (3%)
    pallas_call x1, Pallas kernels, local(): pl.pallas_call(body, out_shape=jax.ShapeDtypeStruct((4, 8, 32, 512), jnp....  95.7 us
    unnamed x1, local copies, waits for them, and re-layouts  3.19 us

profile of v5, /device:TPU:1, one launch (start us, length us, event | category | flops | bytes accessed | tf_op | source)
XLA Modules:
  0.0 98.9 jit_solution(1000163554899712413)
XLA Ops:
  0.0 95.7 %shard_map.17 = f32[4,8,32,512]{3,2,1,0:T(8,128)} custom-call(f32[4,8,32,512]{3,2,1,0:T(8,128)} %bitcast.3), custom_call_target="tpu_custom_call" | custom-call | tf_op jit(solution)/shard_map/pallas_call | solution.py:1063
  95.7 3.2 %copy.3 = f32[32,32,512]{2,1,0:T(8,128)} copy(f32[32,32,512]{2,1,0:T(8,128)} %bitcast.2) | data formatting | bytes 4194304

commit v6 on v3

--- a/solution.py
+++ b/solution.py
@@ -374,8 +374,9 @@
         e = [full[j] + full[q - j] for j in range(half)]
         o = [full[j] - full[q - j] for j in range(half)]
         y = [None] * (q + 1)
+        e = [v - e[0] for v in e[1:]]
         for i in range(half):
-            ev, od = mix(lv.even[i], e), mix(lv.odd[i], o)
+            ev, od = mix(lv.even[i][1:], e), mix(lv.odd[i], o)
             y[i] = od if ev is None else ev + od
             y[q - i] = -od if ev is None else ev - od
         own = jnp.where(first[dim], float(lv.gain[q, q]), 0.0)
@@ -452,7 +453,7 @@
                         t = node(dim, m, i, k)
                         y[t] = got[m] if t not in y else y[t] + got[m]
         drain(name)
-        for dim in ALL_DIMS:
+        for dim in "cba":
             before = load_face(name, dim, -1, n)
             after = load_face(name, dim, 1, n)
             for i in range(n):
@@ -484,13 +485,13 @@
             send_edge(name, dims, 1, [closed[t] for t in plane(dims, n, q)])
         drain(name)
         r = {t: closed[t] for t in itertools.product(range(n), repeat=3)}
-        for dim in ALL_DIMS:
+        for dim in "cba":
             got = load_face(name, dim, 1, n)
             for i in range(n):
                 for k in range(n):
                     t = node(dim, 0, i, k)
                     r[t] = r[t] + got[i][k]
-        for dims in SUBSETS[3:]:
+        for dims in ("bc", "ab", "ac", "abc"):
             receive((name, dims, 1))
             places = plane(dims, n, 0)
             for t, v in zip(places, load_edge(name, dims, 1, len(places))):
@@ -509,7 +510,7 @@
             send_edge(name, dims, -1, [v[t] for t in plane(dims, n, 0)])
         drain(name)
         halo = {}
-        for dim in ALL_DIMS:
+        for dim in "cba":
             got = load_face(name, dim, -1, n)
             for i in range(n):
                 for k in range(n):

time: 97.7 us -> 98 us (level)
  no operation moved by 1% of the time
where the time goes in v6:
time: 98 us; the launch traced here: 97.9 us
  Pallas kernels  95 us (97%)
  local copies, waits for them, and re-layouts  2.91 us (3%)
    pallas_call x1, Pallas kernels, local(): pl.pallas_call(body, out_shape=jax.ShapeDtypeStruct(residual.shape, jnp.f...  95 us
    unnamed x3, local copies, waits for them, and re-layouts  2.91 us

profile of v6, /device:TPU:1, one launch (start us, length us, event | category | flops | bytes accessed | tf_op | source)
XLA Modules:
  0.0 97.9 jit_solution(15646769584142566460)
XLA Ops:
  0.0 0.0 copy-start
  0.0 1.6 %copy-done = f32[32,32,512]{2,1,0:T(8,128)S(1)} copy-done((f32[32,32,512]{2,1,0:T(8,128)S(1)}, f32[32,32,512]{2,1,0:T(8,128)}, u32[]{:S(2)}) %copy-start) | copy-done | bytes 2097176
  1.6 95.0 %shard_map.17 = f32[32,32,512]{2,1,0:T(8,128)S(1)} custom-call(f32[4,8,32,512]{3,2,1,0:T(8,128)S(1)} %bitcast.1), custom_call_target="tpu_custom_call" | custom-call | tf_op jit(solution)/shard_map/pallas_call | solution.py:1055
  96.5 1.3 %copy.3 = f32[32,32,512]{2,1,0:T(8,128)} copy(f32[32,32,512]{2,1,0:T(8,128)S(1)} %shard_map.17) | data formatting | bytes 4194304
Async XLA Ops:
  0.0 1.6 %copy-start = (f32[32,32,512]{2,1,0:T(8,128)S(1)}, f32[32,32,512]{2,1,0:T(8,128)}, u32[]{:S(2)}) copy-start(f32[32,32,512]{2,1,0:T(8,128)} %param.1) | copy-start | bytes 6291460
